TPU v7x, 32 devices: a whole 2x2x4 slice. The times are simulated.
32 devices in a mesh: dp: 8 (over z, x), tensor: 4 (over y, core).
Axes of the slice: x: 2, y: 2, z: 4, core: 2. Of those that a mesh axis runs over, the one named last changes fastest.
Arguments:
- tokens: bfloat16 [8192, 768], P(('dp', 'tensor')), may hold values from -6 to 6
- cotangent: bfloat16 [8192, 768], P(('dp', 'tensor')), may hold values from -6 to 6
- lengths: int32 [8, 4], P('dp'), may hold values from 0 to 1024, as said below
- timesteps: int32 [8, 4], P('dp'), may hold values from 0 to 999
- w_self: bfloat16 [1536, 768], replicated, may hold values from -0.15625 to 0.15625
- ln_gain: float32 [2, 768], replicated, may hold values from 0.5 to 1.5
- ln_bias: float32 [2, 768], replicated, may hold values from -1.8 to 1.8
- w_qkv: bfloat16 [2, 3, 768, 768], P(None, None, None, 'tensor'), may hold values from -0.21875 to 0.21875
- w_out: bfloat16 [2, 768, 768], P(None, 'tensor'), may hold values from -0.875 to 0.875
- w_ada: float32 [2, 768, 1536], replicated, may hold values from -0.21875 to 0.21875
- b_ada: float32 [2, 1536], replicated, may hold values from -1.8 to 1.8
- w_up: bfloat16 [2, 768, 3072], P(None, None, 'tensor'), may hold values from -0.21875 to 0.21875
- w_down: bfloat16 [2, 3072, 768], P(None, 'tensor'), may hold values from -0.109375 to 0.109375
- b_down: float32 [2, 768], replicated, may hold values from -1.8 to 1.8
Outputs:
- activations: bfloat16 [8192, 768], P(('dp', 'tensor'))
- grad_tokens: float32 [8192, 768], P(('dp', 'tensor'))
- grad_ln_gain: float32 [2, 768], replicated
- grad_ln_bias: float32 [2, 768], replicated
- grad_qkv: float32 [2, 3, 768, 768], P(None, None, 'dp', 'tensor')
- grad_out: float32 [2, 768, 768], P(None, 'tensor', 'dp')
- grad_ada: float32 [2, 768, 1536], replicated
- grad_ada_bias: float32 [2, 1536], replicated
- grad_up: float32 [2, 768, 3072], P(None, 'dp', 'tensor')
- grad_down: float32 [2, 3072, 768], P(None, 'tensor', 'dp')
- grad_down_bias: float32 [2, 768], replicated
- grad_self: float32 [1536, 768], replicated
Inputs may be any that keep to these rules, and one draw needn't show every extreme that they name: `lengths`: each row is either one sequence of 1024 tokens followed by zeros, or 4 sequences of 256 tokens; at least one row is of the first kind.
All inputs are finite; a program needn't handle non-finite values.
Results may differ from a plain program's by a relative error of at most 0.018.
Values may be sent and summed in bfloat16 or wider, within the bound.
A program may use at most 192 MiB of HBM per device.

v0:
```python
import functools

import jax
import jax.numpy as jnp
from jax import lax
from jax.experimental import pallas as pl
from jax.experimental.pallas import tpu as pltpu
from jax.sharding import PartitionSpec as P

HD = 64
HALF = HD // 2
BF = jnp.bfloat16
F32 = jnp.float32
MESH = pl.DeviceIdType.MESH
EPS = 1e-05
LIMIT = 60 << 20


def norm(rows):
    centred = rows - jnp.mean(rows, axis=-1, keepdims=True)
    rstd = lax.rsqrt(jnp.mean(centred * centred, axis=-1, keepdims=True) + EPS)
    return (centred * rstd, rstd)


def norm_back(grad, hat, rstd):
    return rstd * (
        grad
        - jnp.mean(grad, axis=-1, keepdims=True)
        - hat * jnp.mean(grad * hat, axis=-1, keepdims=True)
    )


def dot(left, right, dims=((1,), (0,))):
    return lax.dot_general(left, right, (dims, ((), ())), preferred_element_type=F32)


NT = ((1,), (1,))
TN = ((0,), (0,))


def head_mask(head, columns, rotary):
    lane = lax.broadcasted_iota(jnp.int32, (1, columns), 1)
    if rotary:
        return (lane % 128) // HALF == head
    return lane // HD == head


def keep_head(rows, head, rotary):
    return jnp.where(head_mask(head, rows.shape[1], rotary), rows, jnp.zeros_like(rows))


def turned_place(columns, start, total):
    row = lax.broadcasted_iota(jnp.int32, (256, total), 0)
    column = lax.broadcasted_iota(jnp.int32, (256, total), 1) - start
    source = column // HD * HALF + column % HD // HALF * 128 + column % HALF
    fits = (source == row) & (column >= 0) & (column < columns)
    return fits.astype(F32).astype(BF)


def plain_place(columns, start, total):
    row = lax.broadcasted_iota(jnp.int32, (columns, total), 0)
    column = lax.broadcasted_iota(jnp.int32, (columns, total), 1) - start
    return (row == column).astype(F32).astype(BF)


def span(start, size):
    return pl.ds(pl.multiple_of(start, size), size)


class Group:
    def __init__(self, sems, ids, gathered, pair_out, pair_in, own_out, own_in, far_out, far_in):
        self.sems = sems
        self.ids = ids
        self.gathered = gathered
        self.pair_out, self.pair_in = pair_out, pair_in
        self.own_out, self.own_in = own_out, own_in
        self.far_out, self.far_in = far_out, far_in
        self.half = gathered.shape[0] // 8

    def copy(self, src, dst, kind, part, far):
        send, recv = self.sems
        return pltpu.make_async_remote_copy(
            src_ref=src,
            dst_ref=dst,
            send_sem=send.at[kind, part],
            recv_sem=recv.at[kind, part],
            device_id=self.ids[1] if far else self.ids[0],
            device_id_type=MESH,
        )

    def rows(self, start):
        return pl.ds(pl.multiple_of(start, self.half), self.half)

    def pair(self, part):
        return 6 * self.half - 2 * self.half * part

    def far_copy(self, part):
        own = self.gathered.at[self.rows(part * self.half)]
        return self.copy(own, self.gathered.at[self.rows(self.pair(part))], 0, part, True)

    def sibling_copy(self, part):
        own = self.gathered.at[self.rows(part * self.half)]
        place = self.gathered.at[self.rows((2 + part) * self.half)]
        return self.copy(own, place, 1, part, False)

    def forward_copy(self, part):
        src = self.gathered.at[self.rows(self.pair(part))]
        dst = self.gathered.at[self.rows(self.pair(part) + self.half)]
        return self.copy(src, dst, 2, part, False)

    def send(self, part):
        self.far_copy(part).start()
        self.sibling_copy(part).start()

    def receive(self, step):
        @pl.when(step == 1)
        def _():
            self.sibling_copy(0).wait_recv()
            self.sibling_copy(1).wait_recv()

        @pl.when(step >= 2)
        def _():
            part = step - 2
            self.far_copy(part).wait_recv()
            self.forward_copy(part).start()
            self.forward_copy(part).wait()

    def pair_copy(self, part):
        return self.copy(self.pair_out.at[part], self.pair_in.at[part], 3, part, False)

    def own_copy(self):
        return self.copy(self.own_out, self.own_in, 4, 0, False)

    def sum_copy(self, part):
        return self.copy(self.far_out.at[part], self.far_in.at[part], 5, part, True)

    def scatter(self, unit, total, own):
        @pl.when(unit == 0)
        def _():
            own[...] = total[...]

        @pl.when(unit == 1)
        def _():
            self.own_out[...] = total[...].astype(BF)
            self.own_copy().start()

        @pl.when(unit >= 2)
        def _():
            part = 3 - unit
            self.pair_out[part] = total[self.half :, :].astype(BF)
            self.pair_copy(part).start()
            self.pair_copy(part).wait_recv()
            self.far_out[part] = (
                total[: self.half, :] + self.pair_in[part].astype(F32)
            ).astype(BF)
            self.sum_copy(part).start()

    def collect(self, part, own):
        if part == 0:
            self.own_copy().wait_recv()
        self.sum_copy(part).wait_recv()
        rows = pl.ds(part * self.half, self.half)
        return own[rows, :] + self.own_in[rows, :].astype(F32) + self.far_in[part].astype(F32)

    def finish(self):
        for part in range(2):
            self.far_copy(part).wait_send()
            self.sibling_copy(part).wait_send()
            self.pair_copy(part).wait_send()
            self.sum_copy(part).wait_send()
        self.own_copy().wait_send()


def neighbours():
    group = lax.axis_index("dp")
    place = lax.axis_index("tensor")
    core = lax.rem(place, 2)
    return ((group, place + 1 - 2 * core), (group, lax.rem(place + 2, 4)))


class Spot:
    def __init__(self, deep):
        group = lax.axis_index("dp")
        self.place = lax.axis_index("tensor")
        self.deep = deep
        self.z = group // 2
        self.x = lax.rem(group, 2)
        self.across = (2 * self.z + 1 - self.x, self.place)

    def level(self, ahead):
        return lax.rem(self.z + ahead, self.deep)

    def along(self, ahead):
        return (2 * self.level(ahead) + self.x, self.place)

    def partners(self):
        return [self.across] + [self.along(ahead) for ahead in range(1, self.deep)]


def meet(ids):
    barrier = pltpu.get_barrier_semaphore()
    for device in ids:
        pl.semaphore_signal(barrier, inc=1, device_id=device, device_id_type=MESH)
    pl.semaphore_wait(barrier, len(ids))


class DpSum:
    def __init__(self, spot, src, out, scratch):
        self.spot, self.src, self.out = spot, src, out
        self.pairs, self.rest, self.sems = scratch
        self.block = self.pairs.shape[1]

    @staticmethod
    def scratch(deep, block, columns):
        return [
            pltpu.VMEM((deep, block, columns), BF),
            pltpu.VMEM((deep - 1, block, columns), BF),
            pltpu.SemaphoreType.DMA((4, deep)),
        ]

    def rows(self, ahead, x):
        start = (2 * self.spot.level(ahead) + x) * self.block
        return pl.ds(pl.multiple_of(start, self.block), self.block)

    def x_copy(self, ahead):
        return pltpu.make_async_remote_copy(
            src_ref=self.src.at[self.rows(ahead, 1 - self.spot.x)],
            dst_ref=self.pairs.at[ahead],
            send_sem=self.sems.at[0, ahead],
            recv_sem=self.sems.at[1, ahead],
            device_id=self.spot.across,
            device_id_type=MESH,
        )

    def z_copy(self, ahead):
        return pltpu.make_async_remote_copy(
            src_ref=self.pairs.at[ahead],
            dst_ref=self.rest.at[ahead - 1],
            send_sem=self.sems.at[2, ahead],
            recv_sem=self.sems.at[3, ahead],
            device_id=self.spot.along(ahead),
            device_id_type=MESH,
        )

    def order(self):
        return [*range(1, self.spot.deep), 0]

    def start(self):
        for ahead in self.order():
            self.x_copy(ahead).start()

    def middle(self):
        for ahead in self.order():
            self.x_copy(ahead).wait_recv()
            total = self.src[self.rows(ahead, self.spot.x), :].astype(F32)
            total = total + self.pairs[ahead].astype(F32)
            if ahead:
                self.pairs[ahead] = total.astype(BF)
                self.z_copy(ahead).start()
            else:
                self.out[...] = total
        for ahead in self.order():
            self.x_copy(ahead).wait_send()

    def end(self):
        for ahead in range(1, self.spot.deep):
            self.z_copy(ahead).wait_recv()
        total = self.out[...]
        for ahead in range(1, self.spot.deep):
            total = total + self.rest[ahead - 1].astype(F32)
        self.out[...] = total
        for ahead in range(1, self.spot.deep):
            self.z_copy(ahead).wait_send()


def group_scratch(rows, width):
    half = rows // 8
    return [
        pltpu.VMEM((rows, width), BF),
        pltpu.VMEM((2, half, width), BF),
        pltpu.VMEM((2, half, width), BF),
        pltpu.VMEM((2 * half, width), BF),
        pltpu.VMEM((2 * half, width), BF),
        pltpu.VMEM((2, half, width), BF),
        pltpu.VMEM((2, half, width), BF),
    ]


def gelu_parts(hidden):
    cdf = 0.5 * (1.0 + lax.erf(hidden * (0.5**0.5)))
    density = jnp.exp(hidden * hidden * -0.5) * 0.3989422804014327
    return (hidden * cdf, cdf + hidden * density)


def load_turned(wq, wk, wqk):
    turn = turned_place(wq.shape[0], 0, wq.shape[0])
    wqk[:256, :] = dot(turn, wq[...]).astype(BF)
    wqk[256:, :] = dot(turn, wk[...]).astype(BF)


def is_packed(lengths_ref, length):
    return (lengths_ref[:, 0:1] < length).astype(jnp.int32).astype(F32)


def owner(chunk):
    return jnp.where(chunk < 4, chunk // 2, 2 + chunk % 2)


def apart(keys, queries, packed):
    return (keys != queries).astype(jnp.int32).astype(F32) * (packed * -1e9)


def unit_owner(unit, half):
    return jnp.where(unit < 2, unit, 2 + half)


SAVED = ("a", "q", "k", "v", "o", "x1", "m", "g", "slope", "x", "lse")


def forward_kernel(depth, heads, refs):
    refs = list(refs)

    def take(count):
        made = refs[:count]
        del refs[:count]
        return made

    (gain_ref, bias_ref, bdown_ref, bada_ref, lengths_ref, steps_ref) = take(6)
    (rotary_ref, time_ref) = take(2)
    (tokens_hbm, wself_hbm, wqkv_hbm, wout_hbm, wup_hbm, wdown_hbm, wada_hbm) = take(7)
    (acts_ref, est_ref, cond_ref, cos_ref, sin_ref, temb_ref) = take(6)
    saved_hbm = [dict(zip(SAVED, take(len(SAVED)))) for _ in range(depth)]
    (send, recv, send2, recv2, load_sems, store_sems) = take(6)
    (tokens, wself, wada) = take(3)
    weights = [take(6) for _ in range(depth)]
    wqks = take(depth)
    first, second = take(7), take(7)
    (qb, kb, vb, lse, ob, x1, gb, gpb, total, own, xb, start) = take(12)
    ids = neighbours()
    sources = [tokens_hbm, wself_hbm.at[0], wself_hbm.at[1]]
    places = [tokens, wself.at[0], wself.at[1]]
    for layer in range(depth):
        sources += [wqkv_hbm.at[layer, part] for part in range(3)]
        sources += [wout_hbm.at[layer], wup_hbm.at[layer], wdown_hbm.at[layer]]
        places += weights[layer]
    loads = [
        pltpu.make_async_copy(src, dst, load_sems.at[i])
        for i, (src, dst) in enumerate(zip(sources, places))
    ]
    ada_loads = [
        pltpu.make_async_copy(wada_hbm.at[layer], wada, load_sems.at[len(loads)])
        for layer in range(depth)
    ]
    order = [0, 1, *range(3, 9)]
    for i in order:
        loads[i].start()
    ada_loads[0].start()
    for i in range(len(loads)):
        if i not in order:
            loads[i].start()
    meet(ids)
    attn = Group((send, recv), ids, *first)
    feed = Group((send2, recv2), ids, *second)
    abuf, mbuf = first[0], second[0]
    half = attn.half
    unit_rows = 2 * half
    length = 8 * half
    width = xb.shape[1]
    columns = heads * HD
    packed = is_packed(lengths_ref, length)
    buffers = dict(zip(SAVED, (abuf, qb, kb, vb, ob, x1, mbuf, gb, gpb, xb, lse)))
    pending = []

    def store(layer, *names):
        for name in names:
            made = pltpu.make_async_copy(
                buffers[name], saved_hbm[layer][name], store_sems.at[SAVED.index(name)]
            )
            made.start()
            pending.append((name, made))

    def stored(*names):
        for each in list(pending):
            if each[0] in names:
                each[1].wait()
                pending.remove(each)

    def begin(layer, part, rows, values):
        xb[rows, :] = values
        hat = norm(values)[0]
        gain = gain_ref[layer : layer + 1, :]
        abuf[rows, :] = (hat * gain + bias_ref[layer : layer + 1, :]).astype(BF)
        attn.send(part)

    loads[0].wait()
    loads[1].wait()
    for part in range(2):
        rows = pl.ds(part * half, half)
        made = dot(tokens[rows, :], wself[0])
        start[rows, :] = made
        begin(0, part, rows, made)

    def make_tables():
        place = lax.axis_index("tensor")
        sibling = ids[0][1]
        far = ids[1][1]
        far_other = lax.rem(sibling + 2, 4)
        row = lax.broadcasted_iota(jnp.int32, (half, 128), 0).astype(F32)
        for chunk, (block, part) in enumerate(
            zip(
                (place, place, sibling, sibling, far, far_other, far, far_other),
                (0, 1, 0, 1, 1, 1, 0, 0),
            )
        ):
            rows = pl.ds(chunk * half, half)
            offset = (block * unit_rows).astype(F32)
            position = row + part * half + (1.0 - packed) * offset
            angle = position * rotary_ref[...]
            cos_ref[rows, :] = jnp.cos(angle)
            sin_ref[rows, :] = jnp.sin(angle)
        steps = steps_ref[...].astype(F32)
        slot = lax.broadcasted_iota(jnp.int32, steps.shape, 1)
        mine = jnp.sum(jnp.where(slot == place, steps, 0.0), axis=1, keepdims=True)
        step = packed * mine + (1.0 - packed) * steps[:, 0:1]
        angle = jnp.broadcast_to(step * time_ref[...], (8, width // 2))
        temb_ref[:, : width // 2] = jnp.cos(angle)
        temb_ref[:, width // 2 :] = jnp.sin(angle)

    def make_cond(layer):
        ada_loads[layer].wait()
        column = temb_ref[...].T[:, 0:1]
        made = jnp.sum(wada[...] * column, axis=0, keepdims=True)
        made = made + bada_ref[layer : layer + 1, :]
        cond_ref[8 * layer : 8 * layer + 8, :] = jnp.broadcast_to(made, (8, 2 * width))
        if layer + 1 < depth:
            ada_loads[layer + 1].start()

    def run(layer, save, after_layer):
        (wq, wk, wv, wout, wup, wdown) = weights[layer]
        wqk = wqks[layer]
        if not save:
            if layer == 0:
                make_tables()
            for i in range(3 + 6 * layer, 6 + 6 * layer):
                loads[i].wait()
            load_turned(wq, wk, wqk)
        stored("q", "k", "v")

        def project(step, carry):
            attn.receive(step)
            unit = jnp.where(step < 2, step, 5 - step)
            rows = span(unit * unit_rows, unit_rows)
            normed = abuf[rows, :]
            mixed = dot(normed, wqk[...], NT)
            cosine = cos_ref[rows, :]
            sine = sin_ref[rows, :]
            for place, dst, scale in ((0, qb, HD**-0.5), (256, kb, 1.0)):
                first_half = mixed[:, place : place + 128]
                second_half = mixed[:, place + 128 : place + 256]
                dst[rows, :128] = ((first_half * cosine - second_half * sine) * scale).astype(BF)
                dst[rows, 128:] = ((second_half * cosine + first_half * sine) * scale).astype(BF)
            vb[rows, :] = dot(normed, wv[...], NT).astype(BF)
            return carry

        lax.fori_loop(0, 4, project, 0)
        stored("o", "lse", "m", "x1", "g", "slope")
        if save:
            store(layer, "a", "x", "q", "k", "v")
        elif layer == 0:
            for i in (6, 7, 8):
                loads[i].wait()
        else:
            for i in range(6 + 6 * layer, 9 + 6 * layer):
                loads[i].wait()
        lane = lax.broadcasted_iota(jnp.int32, (1, 128), 1)

        def attend(step, carry):
            unit = 3 - step
            rows = span(unit * unit_rows, unit_rows)
            queries = qb[rows, :]
            attended = jnp.zeros((unit_rows, columns), F32)
            logs = jnp.zeros((unit_rows, 128), F32)
            part = lax.broadcasted_iota(jnp.int32, (2, 1, length), 0)
            chunk = lax.broadcasted_iota(jnp.int32, (2, 1, length), 2) // half
            neg = apart(owner(chunk), unit_owner(unit, part), packed.reshape(1, 1, 1))
            for head in range(heads):
                scores = dot(keep_head(queries, head, True), kb[...], NT)
                scores = scores.reshape(2, half, length) + neg
                scores = scores.reshape(unit_rows, length)
                largest = jnp.max(scores, axis=-1, keepdims=True)
                shares = jnp.exp(scores - largest)
                sums = jnp.sum(shares, axis=-1, keepdims=True)
                output = dot(shares.astype(BF), vb[...]) * (1.0 / sums)
                attended = jnp.where(head_mask(head, columns, False), output, attended)
                if save:
                    logs = jnp.where(lane == head, largest + jnp.log(sums), logs)
            if save:
                lse[unit] = logs.T[:8, :]
            attended = attended.astype(BF)
            ob[rows, :] = attended
            total[...] = dot(attended, wout[...])
            attn.scatter(unit, total, own)
            return carry

        lax.fori_loop(0, 4, attend, 0)
        if not save:
            make_cond(layer)
        shift = cond_ref[8 * layer : 8 * layer + 1, :width]
        scale = cond_ref[8 * layer : 8 * layer + 1, width:]
        if save or layer:
            feed.finish()
        for part in range(2):
            rows = pl.ds(part * half, half)
            after = xb[rows, :] + attn.collect(part, own)
            x1[rows, :] = after
            mbuf[rows, :] = (norm(after)[0] * (1.0 + scale) + shift).astype(BF)
            feed.send(part)
        stored("a", "x")
        if save:
            store(layer, "o", "lse", "x1")

        def expand(step, carry):
            feed.receive(step)
            unit = jnp.where(step < 2, step, 5 - step)
            rows = span(unit * unit_rows, unit_rows)
            hidden = dot(mbuf[rows, :], wup[...])
            gated, slope = gelu_parts(hidden)
            gated = gated.astype(BF)
            if save:
                gb[rows, :] = gated
                gpb[rows, :] = slope.astype(BF)
            total[...] = dot(gated, wdown[...])
            feed.scatter(unit, total, own)
            return carry

        lax.fori_loop(0, 4, expand, 0)
        if save:
            store(layer, "m", "g", "slope")
        attn.finish()
        for part in range(2):
            rows = pl.ds(part * half, half)
            made = x1[rows, :] + feed.collect(part, own) + bdown_ref[layer : layer + 1, :]
            after_layer(part, rows, made)

    def between(part, rows, made):
        estimate = made.astype(BF)
        est_ref[rows, :] = estimate
        begin(0, part, rows, start[rows, :] + dot(estimate, wself[1]))

    def close(part, rows, made):
        acts_ref[rows, :] = made.astype(BF)

    for save in (False, True):
        for layer in range(depth):
            if layer + 1 < depth:
                run(layer, save, functools.partial(begin, layer + 1))
            elif save:
                run(layer, save, close)
            else:
                loads[2].wait()
                run(layer, save, between)
    feed.finish()
    stored(*SAVED)


def any_spec():
    return pl.BlockSpec(memory_space=pl.ANY)


def vmem_spec():
    return pl.BlockSpec(memory_space=pltpu.VMEM)


def forward(heads, tokens, w_self, vectors, weights):
    depth = weights[0].shape[0]
    block, width = tokens.shape
    length = 4 * block
    columns = heads * HD
    units = weights[2].shape[2]
    lanes = jnp.arange(128) % HALF
    rotary = jnp.exp(-jnp.log(10000.0) * lanes.astype(F32) / HALF)[None]
    halves = jnp.arange(width // 2).astype(F32)
    times = jnp.exp(-jnp.log(10000.0) * halves / (width // 2))[None]
    kept = {
        "a": ((length, width), BF),
        "q": ((length, 256), BF),
        "k": ((length, 256), BF),
        "v": ((length, columns), BF),
        "o": ((length, columns), BF),
        "x1": ((block, width), F32),
        "m": ((length, width), BF),
        "g": ((length, units), BF),
        "slope": ((length, units), BF),
        "x": ((block, width), F32),
        "lse": ((4, 8, block), F32),
    }
    kept_shapes = [jax.ShapeDtypeStruct(*kept[name]) for name in SAVED]
    out_shape = [
        jax.ShapeDtypeStruct((block, width), BF),
        jax.ShapeDtypeStruct((block, width), BF),
        jax.ShapeDtypeStruct((8 * depth, 2 * width), F32),
        jax.ShapeDtypeStruct((length, 128), F32),
        jax.ShapeDtypeStruct((length, 128), F32),
        jax.ShapeDtypeStruct((8, width), F32),
    ] + kept_shapes * depth
    out_specs = [vmem_spec()] * 6 + [any_spec()] * (depth * len(SAVED))
    scratch = [pltpu.SemaphoreType.DMA((6, 2))] * 4
    scratch += [
        pltpu.SemaphoreType.DMA((4 + 6 * depth,)),
        pltpu.SemaphoreType.DMA((len(SAVED),)),
        pltpu.VMEM((block, width), BF),
        pltpu.VMEM((2, width, width), BF),
        pltpu.VMEM((width, 2 * width), F32),
    ]
    for _ in range(depth):
        scratch += [pltpu.VMEM((columns, width), BF)] * 3
        scratch += [pltpu.VMEM(each.shape[1:], BF) for each in weights[1:4]]
    scratch += [pltpu.VMEM((512, width), BF)] * depth
    scratch += group_scratch(length, width) + group_scratch(length, width)
    for name in ("q", "k", "v", "lse", "o", "x1", "g", "slope"):
        scratch.append(pltpu.VMEM(*kept[name]))
    scratch += [pltpu.VMEM((block, width), F32)] * 4

    def kernel(*refs):
        forward_kernel(depth, heads, refs)

    operands = [*vectors, rotary, times]
    remote = [tokens, w_self.reshape(2, width, width), *weights]
    made = pl.pallas_call(
        kernel,
        out_shape=out_shape,
        in_specs=[vmem_spec()] * len(operands) + [any_spec()] * len(remote),
        out_specs=out_specs,
        scratch_shapes=scratch,
        compiler_params=pltpu.CompilerParams(
            collective_id=1, has_side_effects=True, vmem_limit_bytes=LIMIT
        ),
        name="layers_forward",
    )(*operands, *remote)
    count = len(SAVED)
    saved = [made[6 + count * layer : 6 + count * (layer + 1)] for layer in range(depth)]
    return (made[:6], [dict(zip(SAVED, each)) for each in saved])


class Ladder:
    def __init__(self, sems):
        self.send, self.recv = sems
        self.used = 0
        self.open = []

    def copy(self, src, dst, device):
        made = pltpu.make_async_remote_copy(
            src_ref=src,
            dst_ref=dst,
            send_sem=self.send.at[self.used],
            recv_sem=self.recv.at[self.used],
            device_id=device,
            device_id_type=MESH,
        )
        self.used += 1
        assert self.used <= LADDER_COPIES
        made.start()
        self.open.append(made)
        return made

    def finish(self):
        for each in self.open:
            each.wait_send()


LADDER_COPIES = 34


class Loads:
    def __init__(self, sems):
        self.sems = sems
        self.names = {}

    def add(self, name, sources, buffer):
        self.names[name] = (sources, buffer, len(self.names))
        return buffer

    def copy(self, name, layer):
        sources, buffer, place = self.names[name]
        return pltpu.make_async_copy(sources[layer], buffer, self.sems.at[place])

    def start(self, layer, *names):
        if layer >= 0:
            for name in names:
                self.copy(name, layer).start()

    def wait(self, layer, *names):
        for name in names:
            self.copy(name, layer).wait()


def backward_kernel(depth, heads, deep, refs):
    refs = list(refs)

    def take(count):
        made = refs[:count]
        del refs[:count]
        return made

    cot_ref, gain_ref, lengths_ref, cos_ref, sin_ref, temb_ref, cond_ref = take(7)
    joined_hbm = take(2)
    wqkv_hbm, wout_hbm, wup_hbm, wdown_hbm, _ = take(5)
    saved_hbm = [dict(zip(SAVED, take(len(SAVED)))) for _ in range(depth)]
    (out_ref, small_ref) = take(2)
    attn_outs, feed_outs = take(depth), take(depth)
    if deep:
        sum_ref, vec_ref = take(2)
    send, recv, send2, recv2, load_sems, store_sems = take(6)
    loads = Loads(load_sems)
    wq, wk, wv = (
        loads.add(name, [wqkv_hbm.at[layer, part] for layer in range(depth)], take(1)[0])
        for part, name in enumerate(("wq", "wk", "wv"))
    )
    wout, wup, wdown = (
        loads.add(name, [src.at[layer] for layer in range(depth)], take(1)[0])
        for name, src in (("wout", wout_hbm), ("wup", wup_hbm), ("wdown", wdown_hbm))
    )
    abuf, qb, kb, vb, ob, x1b, mbuf, gb, gpb, xb, lse = (
        loads.add(name, [saved_hbm[layer][name] for layer in range(depth)], take(1)[0])
        for name in SAVED
    )
    first = take(7)
    second = take(7)
    (wqk, dhb, qmask, domask, dsb, pb, dkb, dvb, dqk, dvv, work, dxb) = take(12)
    (feed_grads, attn_grads) = take(2)
    ids = neighbours()
    sums = {}
    if deep:
        spot = Spot(deep)
        meet([*ids, *spot.partners()])
        for layer in range(depth):
            for name, src, out in (
                ("up", feed_grads.at[0], feed_outs[layer].at[0]),
                ("down", feed_grads.at[1], feed_outs[layer].at[1]),
                ("attn", attn_grads, attn_outs[layer]),
            ):
                sums[name, layer] = DpSum(spot, src, out, take(3))
        tail_refs = take(10)
        joined = tail_refs[0]
        joined_loads = [
            pltpu.make_async_copy(src, joined.at[i], store_sems.at[i])
            for i, src in enumerate(joined_hbm)
        ]
        for each in joined_loads:
            each.start()
    else:
        meet(ids)
    feed = Group((send, recv), ids, *first)
    attn = Group((send2, recv2), ids, *second)
    ebuf, fbuf = first[0], second[0]
    half = feed.half
    unit_rows = 2 * half
    width = cot_ref.shape[1]
    columns = heads * HD
    tiles = width // 256
    total, own, dx1 = (work.at[pl.ds(i * unit_rows, unit_rows)] for i in range(3))
    top = depth - 1
    packed = is_packed(lengths_ref, 8 * half)
    for part in range(2):
        rows = pl.ds(part * half, half)
        ebuf[rows, :] = cot_ref[rows, :]
        feed.send(part)
    loads.start(top, "wdown", "slope", "wup", "m", "g", "x1", "wout", "q", "k", "v", "lse")
    loads.start(top, "wq", "wk", "wv", "a", "o", "x")
    dxb[...] = cot_ref[...].astype(F32)
    small_ref[...] = jnp.zeros_like(small_ref)

    def outer(left, right, dst):
        def tile(index, carry):
            place = span(index * 256, 256)
            dst[place, :] = dot(left[:, place], right[...], TN).astype(BF)
            return carry

        lax.fori_loop(0, tiles, tile, 0)

    def turn_back(grad, rows, scale):
        cosine = cos_ref[rows, :]
        sine = sin_ref[rows, :]
        first_half = grad[:, :128]
        second_half = grad[:, 128:]
        return (
            ((first_half * cosine + second_half * sine) * scale).astype(BF),
            ((second_half * cosine - first_half * sine) * scale).astype(BF),
        )

    def event(name, layer, kind):
        if (name, layer) in sums:
            getattr(sums[name, layer], kind)()

    for layer in reversed(range(depth)):
        def note(row, value):
            small_ref[8 * layer + row : 8 * layer + row + 1, :] = value

        note(4, jnp.sum(dxb[...], axis=0, keepdims=True))
        dkb[...] = jnp.zeros_like(dkb)
        dvb[...] = jnp.zeros_like(dvb)
        loads.wait(layer, "wdown", "slope", "wup")

        def contract(step, carry):
            feed.receive(step)
            unit = jnp.where(step < 2, step, 5 - step)
            rows = span(unit * unit_rows, unit_rows)
            grad = dot(ebuf[rows, :], wdown[...], NT)
            grad = (grad * gpb[rows, :].astype(F32)).astype(BF)
            dhb[rows, :] = grad
            total[...] = dot(grad, wup[...], NT)
            feed.scatter(unit, total, own)
            return carry

        lax.fori_loop(0, 4, contract, 0)
        loads.start(layer - 1, "wdown", "slope", "wup")
        event("attn", layer + 1, "middle")
        event("up", layer + 1, "end")
        if layer < top:
            attn.finish()
        shift_sum = jnp.zeros((1, width), F32)
        scale_sum = jnp.zeros((1, width), F32)
        for part in range(2):
            if part == 0:
                loads.wait(layer, "m", "x1")
                outer(mbuf, dhb, feed_grads.at[0])
                event("up", layer, "start")
            else:
                loads.wait(layer, "g")
                outer(ebuf, gb, feed_grads.at[1])
                event("down", layer, "start")
            rows = pl.ds(part * half, half)
            grad = feed.collect(part, own)
            hat, rstd = norm(x1b[rows, :])
            shift_sum += jnp.sum(grad, axis=0, keepdims=True)
            scale_sum += jnp.sum(grad * hat, axis=0, keepdims=True)
            after = dxb[rows, :]
            after = after + norm_back(grad * (1.0 + cond_ref[8 * layer : 8 * layer + 1, width:]), hat, rstd)
            dx1[rows, :] = after
            fbuf[rows, :] = after.astype(BF)
            attn.send(part)
        note(0, shift_sum)
        note(1, scale_sum)
        loads.start(layer - 1, "m", "g", "x1")
        loads.wait(layer, "wout", "q", "k", "v", "lse")

        def attend(step, carry):
            attn.receive(step)
            unit = jnp.where(step < 2, step, 5 - step)
            rows = span(unit * unit_rows, unit_rows)
            grad_out = dot(fbuf[rows, :], wout[...], NT).astype(BF)
            queries = qb[rows, :]
            grad_queries = jnp.zeros((unit_rows, 256), F32)
            chunk = lax.broadcasted_iota(jnp.int32, (8, 1, unit_rows), 0)
            part = lax.broadcasted_iota(jnp.int32, (8, 1, unit_rows), 2) // half
            neg = apart(owner(chunk), unit_owner(unit, part), packed.reshape(1, 1, 1))
            for head in range(heads):
                place = pl.ds(head * unit_rows, unit_rows)
                masked = keep_head(queries, head, True)
                masked_out = keep_head(grad_out, head, False)
                qmask[place, :] = masked
                domask[place, :] = masked_out
                scores = dot(kb[...], masked, NT).reshape(8, half, unit_rows)
                shares = jnp.exp(scores - (lse[unit, head : head + 1, :] - neg))
                shares = shares.reshape(8 * half, unit_rows)
                grad_shares = dot(vb[...], masked_out, NT)
                centre = jnp.sum(shares * grad_shares, axis=0, keepdims=True)
                grad_scores = (shares * (grad_shares - centre)).astype(BF)
                pb[:, place] = shares.astype(BF)
                dsb[:, place] = grad_scores
                grad_queries = grad_queries + dot(grad_scores, keep_head(kb[...], head, True), TN)
            dkb[...] += dot(dsb[...], qmask[...])
            dvb[...] += dot(pb[...], domask[...])
            low, high = turn_back(grad_queries, rows, HD**-0.5)
            dqk[rows, :128] = low
            dqk[rows, 128:256] = high
            return carry

        lax.fori_loop(0, 4, attend, 0)
        loads.start(layer - 1, "wout", "q", "k", "v", "lse")
        event("down", layer + 1, "end")
        event("attn", layer + 1, "end")
        event("up", layer, "middle")
        loads.wait(layer, "wq", "wk", "wv")
        load_turned(wq, wk, wqk)

        def spread(step, carry):
            unit = 3 - step
            rows = span(unit * unit_rows, unit_rows)
            low, high = turn_back(dkb[rows, :], rows, 1.0)
            dqk[rows, 256:384] = low
            dqk[rows, 384:512] = high
            values = dvb[rows, :].astype(BF)
            dvv[rows, :] = values
            total[...] = dot(dqk[rows, :], wqk[...]) + dot(values, wv[...])
            attn.scatter(unit, total, own)
            return carry

        lax.fori_loop(0, 4, spread, 0)
        loads.start(layer - 1, "wq", "wk", "wv")
        event("down", layer, "middle")
        loads.wait(layer, "a", "o")
        places = (
            turned_place(columns, 0, 4 * columns),
            turned_place(columns, columns, 4 * columns),
            plain_place(columns, 2 * columns, 4 * columns),
            plain_place(columns, 3 * columns, 4 * columns),
        )

        def attn_tile(index, carry):
            place = span(index * 256, 256)
            normed = abuf[:, place]
            both = dot(normed, dqk[...], TN).astype(BF)
            made = dot(both[:, :256], places[0]) + dot(both[:, 256:], places[1])
            made = made + dot(dot(normed, dvv[...], TN).astype(BF), places[2])
            outs = dot(fbuf[:, place], ob[...], TN).astype(BF)
            attn_grads[place, :] = (made + dot(outs, places[3])).astype(BF)
            return carry

        lax.fori_loop(0, tiles, attn_tile, 0)
        loads.start(layer - 1, "a", "o")
        event("attn", layer, "start")
        if not deep:
            stores = [
                pltpu.make_async_copy(attn_grads, attn_outs[layer], store_sems.at[0]),
                pltpu.make_async_copy(feed_grads, feed_outs[layer], store_sems.at[1]),
            ]
            for each in stores:
                each.start()
            for each in stores:
                each.wait()
        feed.finish()
        loads.wait(layer, "x")
        gain_sum = jnp.zeros((1, width), F32)
        bias_sum = jnp.zeros((1, width), F32)
        for part in range(2):
            rows = pl.ds(part * half, half)
            grad = attn.collect(part, own)
            hat, rstd = norm(xb[rows, :])
            gain_sum += jnp.sum(grad * hat, axis=0, keepdims=True)
            bias_sum += jnp.sum(grad, axis=0, keepdims=True)
            made = dx1[rows, :] + norm_back(
                grad * gain_ref[layer : layer + 1, :], hat, rstd
            )
            dxb[rows, :] = made
            if layer:
                ebuf[rows, :] = made.astype(BF)
                feed.send(part)
        note(2, gain_sum)
        note(3, bias_sum)
        loads.start(layer - 1, "x")
    out_ref[...] = dxb[...]
    if deep:
        for each in joined_loads:
            each.wait()
        tail(deep, spot, ids, sums, dxb, small_ref, temb_ref, work, dsb, tail_refs,
             sum_ref, vec_ref, store_sems)
    attn.finish()


def tail(deep, spot, ids, sums, dxb, small_ref, temb_ref, work, dsb, scratch, sum_ref, vec_ref,
         store_sems):
    (joined, ebuf, jbuf, near_in, next_in, z_in, result, vecs, send, recv) = scratch
    sibling, far = ids
    place = lax.axis_index("tensor")
    core = lax.rem(place, 2)
    y = place // 2
    x, z = spot.x, spot.z
    width = dxb.shape[1]
    ladder = Ladder((send, recv))
    ebuf[0] = dxb[...].astype(BF)
    rows_copy = ladder.copy(ebuf.at[0], ebuf.at[1], sibling)
    joined_copy = ladder.copy(joined.at[1 - core], jbuf, sibling)
    mine = vecs.at[core, y, x, z]
    row = lax.broadcasted_iota(jnp.int32, small_ref.shape, 0)
    mine[...] = jnp.where(row == 5, temb_ref[0:1, :], small_ref[...]).astype(BF)
    vec_z = [ladder.copy(mine, mine, spot.along(ahead)) for ahead in range(1, deep)]
    rows_copy.wait_recv()
    joined_copy.wait_recv()
    rest = width // 2

    def tile(index, carry):
        rows = span(index * 256, 256)
        made = dot(joined[core, :, rows], ebuf[0], TN)
        work[rows, :] = made + dot(jbuf[:, rows], ebuf[1], TN)
        return carry

    lax.fori_loop(0, width // 256, tile, 0)
    half, quarter = width // 2, width // 4
    piece = quarter // deep
    ways = (((far, y), (spot.across, x)), ((spot.across, x), (far, y)))
    lanes = (pl.ds(0, rest), pl.ds(rest, rest))
    firsts = []
    for side, ((device, bit), _) in enumerate(ways):
        out = dsb.at[pl.ds(0, half), lanes[side]]
        out[...] = work[span((1 - bit) * half, half), lanes[side]].astype(BF)
        firsts.append(ladder.copy(out, near_in.at[side], device))
    for each in vec_z:
        each.wait_recv()
    row_z = vecs.at[core, y, x]
    vec_x = ladder.copy(row_z, row_z, spot.across)
    seconds = []
    for side, ((_, bit), (device, bit2)) in enumerate(ways):
        firsts[side].wait_recv()
        kept = work.at[span(bit * half, half), lanes[side]]
        kept[...] = kept[...] + near_in[side].astype(F32)
        out = dsb.at[pl.ds(half, quarter), lanes[side]]
        out[...] = work[span(bit * half + (1 - bit2) * quarter, quarter), lanes[side]].astype(BF)
        seconds.append(ladder.copy(out, next_in.at[side], device))
    vec_x.wait_recv()
    plane = vecs.at[core, y]
    vec_y = ladder.copy(plane, plane, far)
    sums["attn", 0].middle()
    thirds = []
    for side, ((_, bit), (_, bit2)) in enumerate(ways):
        seconds[side].wait_recv()
        kept = work.at[span(bit * half + bit2 * quarter, quarter), lanes[side]]
        kept[...] = kept[...] + next_in[side].astype(F32)
        out = dsb.at[pl.ds(half + quarter, quarter), lanes[side]]
        out[...] = kept[...].astype(BF)
        for ahead in range(1, deep):
            start = half + quarter + spot.level(ahead) * piece
            thirds.append(
                ladder.copy(
                    dsb.at[span(start, piece), lanes[side]],
                    z_in.at[side, ahead - 1],
                    spot.along(ahead),
                )
            )
    sums["up", 0].end()
    sums["down", 0].end()
    vec_y.wait_recv()
    every = vecs.at[core]
    vec_core = ladder.copy(every, every, sibling)
    lasts = []
    for side, ((_, bit), (_, bit2)) in enumerate(ways):
        for ahead in range(1, deep):
            thirds[side * (deep - 1) + ahead - 1].wait_recv()
        start = bit * half + bit2 * quarter + z * piece
        made = work[span(start, piece), lanes[side]]
        for ahead in range(1, deep):
            made = made + z_in[side, ahead - 1].astype(F32)
        own = result.at[core, side, span(start, piece)]
        own[...] = made.astype(BF)
        lasts += [ladder.copy(own, own, spot.along(ahead)) for ahead in range(1, deep)]
    backs = []
    for side, ((_, bit), (device, bit2)) in enumerate(ways):
        for ahead in range(1, deep):
            lasts[side * (deep - 1) + ahead - 1].wait_recv()
        own = result.at[core, side, span(bit * half + bit2 * quarter, quarter)]
        backs.append(ladder.copy(own, own, device))
    ends = []
    for side, ((device, bit), _) in enumerate(ways):
        backs[side].wait_recv()
        own = result.at[core, side, span(bit * half, half)]
        ends.append(ladder.copy(own, own, device))
    sums["attn", 0].end()
    vec_core.wait_recv()
    vec_store = pltpu.make_async_copy(vecs, vec_ref, store_sems.at[0])
    vec_store.start()
    for each in ends:
        each.wait_recv()
    whole = ladder.copy(result.at[core], result.at[core], sibling)
    whole.wait_recv()
    sum_store = pltpu.make_async_copy(result, sum_ref, store_sems.at[1])
    sum_store.start()
    ladder.finish()
    vec_store.wait()
    sum_store.wait()


def backward(heads, deep, cotangent, gains, lengths, tables, weights, kept, joined):
    depth = len(kept)
    block, width = cotangent.shape
    length = 4 * block
    units = weights[2].shape[2]
    columns = heads * HD
    part = width // (2 * deep) if deep else width
    half, quarter = width // 2, width // 4
    held = [[each[name] for name in SAVED] for each in kept]
    scratch = [pltpu.SemaphoreType.DMA((6, 2))] * 4
    scratch += [pltpu.SemaphoreType.DMA((6 + len(SAVED),)), pltpu.SemaphoreType.DMA((2,))]
    scratch += [pltpu.VMEM((columns, width), BF)] * 3
    scratch += [pltpu.VMEM(each.shape[1:], BF) for each in weights[1:4]]
    scratch += [pltpu.VMEM(each.shape, each.dtype) for each in held[0]]
    scratch += group_scratch(length, width) + group_scratch(length, width)
    scratch += [
        pltpu.VMEM((512, width), BF),
        pltpu.VMEM((length, units), BF),
        pltpu.VMEM((heads * block, 256), BF),
        pltpu.VMEM((heads * block, columns), BF),
        pltpu.VMEM((length, heads * block), BF),
        pltpu.VMEM((length, heads * block), BF),
        pltpu.VMEM((length, 256), F32),
        pltpu.VMEM((length, columns), F32),
        pltpu.VMEM((length, 512), BF),
        pltpu.VMEM((length, columns), BF),
        pltpu.VMEM((3 * block, width), F32),
        pltpu.VMEM((block, width), F32),
        pltpu.VMEM((2, width, units), BF),
        pltpu.VMEM((width, 4 * columns), BF),
    ]
    out_shape = [
        jax.ShapeDtypeStruct((block, width), F32),
        jax.ShapeDtypeStruct((8 * depth, width), F32),
    ]
    kind = F32 if deep else BF
    out_shape += [jax.ShapeDtypeStruct((part, 4 * columns), kind)] * depth
    out_shape += [jax.ShapeDtypeStruct((2, part, units), kind)] * depth
    out_specs = [vmem_spec()] * 2 + [vmem_spec() if deep else any_spec()] * (2 * depth)
    if deep:
        for _ in range(depth):
            scratch += DpSum.scratch(deep, part, units) + DpSum.scratch(deep, part, units)
            scratch += DpSum.scratch(deep, part, 4 * columns)
        vec_shape = (2, 2, 2, deep, 8 * depth, width)
        scratch += [
            pltpu.VMEM((2, block, width), BF),
            pltpu.VMEM((2, block, width), BF),
            pltpu.VMEM((block, width), BF),
            pltpu.VMEM((2, half, half), BF),
            pltpu.VMEM((2, quarter, half), BF),
            pltpu.VMEM((2, deep - 1, quarter // deep, half), BF),
            pltpu.VMEM((2, 2, width, half), BF),
            pltpu.VMEM(vec_shape, BF),
            pltpu.SemaphoreType.DMA((LADDER_COPIES,)),
            pltpu.SemaphoreType.DMA((LADDER_COPIES,)),
        ]
        out_shape += [
            jax.ShapeDtypeStruct((2, 2, width, half), BF),
            jax.ShapeDtypeStruct(vec_shape, BF),
        ]
        out_specs += [any_spec(), any_spec()]

    def kernel(*refs):
        backward_kernel(depth, heads, deep, refs)

    operands = [cotangent, gains, lengths, *tables]
    in_specs = [vmem_spec()] * len(operands)
    remote = [*joined, *weights, *[each for layer in held for each in layer]]
    in_specs += [any_spec()] * len(remote)
    return pl.pallas_call(
        kernel,
        out_shape=out_shape,
        in_specs=in_specs,
        out_specs=out_specs,
        scratch_shapes=scratch,
        compiler_params=pltpu.CompilerParams(
            collective_id=9, has_side_effects=True, vmem_limit_bytes=LIMIT
        ),
        name="layers_backward",
    )(*operands, *remote)


def finish_kernel(depth, refs):
    (low_ref, wself_ref, sum_ref, vec_ref) = refs[:4]
    attn_refs = refs[4 : 4 + depth]
    feed_refs = refs[4 + depth : 4 + 2 * depth]
    (tokens_ref, gain_ref, bias_ref, bada_ref, bdown_ref) = refs[4 + 2 * depth : 9 + 2 * depth]
    (qkv_ref, out_ref, ada_ref, up_ref, down_ref, self_ref) = refs[9 + 2 * depth :]
    step = pl.program_id(0)
    members = vec_ref.shape[0] // (8 * depth)
    width = vec_ref.shape[1]

    def pick(row):
        device = lax.broadcasted_iota(jnp.int32, (members, vec_ref.shape[0]), 0)
        column = lax.broadcasted_iota(jnp.int32, (members, vec_ref.shape[0]), 1)
        wanted = (column == device * 8 * depth + row).astype(F32).astype(BF)
        return dot(wanted, vec_ref[...]).astype(BF)

    rows = ada_ref.shape[1]
    times = pick(5)
    device = lax.broadcasted_iota(jnp.int32, (width, rows), 0)
    column = lax.broadcasted_iota(jnp.int32, (width, rows), 1)
    chosen = (device == column + step * rows).astype(F32).astype(BF)
    times = dot(times, chosen).astype(BF)
    for layer in range(depth):
        for place in range(2):
            ada_ref[layer, :, place * width : (place + 1) * width] = dot(
                times, pick(8 * layer + place), TN
            )
    self_ref[:, : width // 2] = sum_ref[0].astype(F32)
    self_ref[:, width // 2 :] = sum_ref[1].astype(F32)

    @pl.when(step == 0)
    def _():
        row = lax.broadcasted_iota(jnp.int32, (8 * depth, vec_ref.shape[0]), 0)
        column = lax.broadcasted_iota(jnp.int32, (8 * depth, vec_ref.shape[0]), 1)
        ones = (column % (8 * depth) == row).astype(F32).astype(BF)
        totals = dot(ones, vec_ref[...])
        for layer in range(depth):
            here = slice(layer, layer + 1)
            base = 8 * layer
            bada_ref[here, :width] = totals[base : base + 1]
            bada_ref[here, width:] = totals[base + 1 : base + 2]
            gain_ref[here, :] = totals[base + 2 : base + 3]
            bias_ref[here, :] = totals[base + 3 : base + 4]
            bdown_ref[here, :] = totals[base + 4 : base + 5]

    @pl.when(step == 1)
    def _():
        tokens_ref[...] = dot(low_ref[...].astype(BF), wself_ref[...], NT)

    @pl.when(step == 2)
    def _():
        for layer in range(depth):
            grads = attn_refs[layer][...]
            columns = grads.shape[1] // 4
            for place in range(3):
                qkv_ref[layer, place] = grads[:, place * columns : (place + 1) * columns]
            out_ref[layer] = grads[:, 3 * columns :].T

    @pl.when(step == 3)
    def _():
        for layer in range(depth):
            up_ref[layer] = feed_refs[layer][0]
            down_ref[layer] = feed_refs[layer][1]


def finish(depth, low, w_self, sums, vectors, attn_shards, feed_shards):
    block, width = low.shape
    part, columns = attn_shards[0].shape
    columns //= 4
    units = feed_shards[0].shape[2]
    steps = 4
    rows = 2 * width // steps

    def fixed(*shape):
        return pl.BlockSpec(shape, lambda step: (0,) * len(shape))

    def kernel(*refs):
        finish_kernel(depth, refs)

    fixed_shapes = [
        (block, width),
        (depth, width),
        (depth, width),
        (depth, 2 * width),
        (depth, width),
        (depth, 3, part, columns),
        (depth, columns, part),
    ]
    shard = (depth, part, units)
    return pl.pallas_call(
        kernel,
        grid=(steps,),
        out_shape=[
            *[jax.ShapeDtypeStruct(each, F32) for each in fixed_shapes],
            jax.ShapeDtypeStruct((depth, width, 2 * width), F32),
            jax.ShapeDtypeStruct(shard, F32),
            jax.ShapeDtypeStruct(shard, F32),
            jax.ShapeDtypeStruct((2 * width, width), F32),
        ],
        in_specs=[
            fixed(block, width),
            fixed(width, width),
            pl.BlockSpec((None, 2, rows, width // 2), lambda step: (step // 2, 0, step % 2, 0)),
            fixed(*vectors.shape),
            *[fixed(*each.shape) for each in attn_shards],
            *[fixed(*each.shape) for each in feed_shards],
        ],
        out_specs=[
            *[fixed(*each) for each in fixed_shapes],
            pl.BlockSpec((depth, width // steps, 2 * width), lambda step: (0, step, 0)),
            fixed(*shard),
            fixed(*shard),
            pl.BlockSpec((rows, width), lambda step: (step, 0)),
        ],
        compiler_params=pltpu.CompilerParams(vmem_limit_bytes=LIMIT),
        name="write_grads",
    )(low, w_self, sums, vectors, *attn_shards, *feed_shards)


def local(
    tokens,
    cotangent,
    lengths,
    timesteps,
    w_self,
    ln_gain,
    ln_bias,
    w_qkv,
    w_out,
    w_ada,
    b_ada,
    w_up,
    w_down,
    b_down,
):
    width = tokens.shape[1]
    depth = w_qkv.shape[0]
    heads = w_qkv.shape[3] // HD
    deep = 4 if lax.axis_size("dp") == 8 else 0
    weights = (jnp.swapaxes(w_qkv, 2, 3), w_out, w_up, w_down, w_ada)
    vectors = (ln_gain, ln_bias, b_down, b_ada, lengths, timesteps)
    made, kept = forward(heads, tokens, w_self, vectors, weights)
    (activations, estimate, conds, cosine, sine, temb) = made
    made = backward(
        heads,
        deep,
        cotangent,
        ln_gain,
        lengths,
        (cosine, sine, temb, conds),
        weights,
        kept,
        (tokens, estimate),
    )
    grad_rows, smalls = made[:2]
    attn_shards = made[2 : 2 + depth]
    feed_shards = made[2 + depth : 2 + 2 * depth]
    if deep:
        sums, vectors = made[2 + 2 * depth :]
        vectors = vectors.reshape(-1, width)
    else:
        attn_shards = [
            lax.psum_scatter(each, "dp", scatter_dimension=0, tiled=True).astype(F32)
            for each in attn_shards
        ]
        feed_shards = [
            lax.psum_scatter(each, "dp", scatter_dimension=1, tiled=True).astype(F32)
            for each in feed_shards
        ]
        joined = jnp.concatenate([tokens, estimate], axis=1)
        sums = lax.psum(dot(joined, grad_rows.astype(BF), TN).astype(BF), ("dp", "tensor"))
        sums = sums.reshape(2, width, 2, width // 2).swapaxes(1, 2)
        vectors = smalls.at[5].set(temb[0]).astype(BF)
        vectors = lax.all_gather(vectors, ("dp", "tensor"), axis=0, tiled=True)
    made = finish(depth, grad_rows, w_self, sums, vectors, attn_shards, feed_shards)
    (grad_tokens, gain, bias, bias_ada, bias_down, qkv, out, ada, up, down, own) = made
    return (
        activations,
        grad_tokens,
        gain,
        bias,
        qkv,
        out,
        ada,
        bias_ada,
        up,
        jnp.swapaxes(down, 1, 2),
        bias_down,
        own,
    )


def solution(mesh):
    return jax.shard_map(
        local,
        mesh=mesh,
        in_specs=(
            P(("dp", "tensor"), None),
            P(("dp", "tensor"), None),
            P("dp", None),
            P("dp", None),
            P(),
            P(),
            P(),
            P(None, None, None, "tensor"),
            P(None, "tensor", None),
            P(),
            P(),
            P(None, None, "tensor"),
            P(None, "tensor", None),
            P(),
        ),
        out_specs=(
            P(("dp", "tensor"), None),
            P(("dp", "tensor"), None),
            P(),
            P(),
            P(None, None, "dp", "tensor"),
            P(None, "tensor", "dp"),
            P(),
            P(),
            P(None, "dp", "tensor"),
            P(None, "tensor", "dp"),
            P(),
            P(),
        ),
        check_vma=False,
    )
```

profile of v0, /device:TPU:5, one launch (start us, length us, event | category | flops | bytes accessed | tf_op | source)
XLA Modules:
  0.0 358.6 jit_solution(7760249954100488665)
XLA Ops:
  0.6 0.5 fusion.2.refs_6_
  1.2 0.6 multiply_exponential_fusion.refs_7_
  1.7 173.8 %layers_forward.1 = (bf16[256,768]{1,0:T(8,128)(2,1)}, bf16[256,768]{1,0:T(8,128)(2,1)}, f32[16,1536]{1,0:T(8,128)}, f32[1024,128]{1,0:T(8,128)}, f32[1024,128]{...) custom-call(f32[2,768]{1,0:T(2,128)} %refs_1_.4, ...), custom_call_target="tpu_custom_call" | custom-call | tf_op jit(solution)/shard_map/layers_forward/pallas_call | solution.py:629
  175.5 169.9 %layers_backward.1 = (f32[256,768]{1,0:T(8,128)}, f32[16,768]{1,0:T(8,128)}, f32[96,768]{1,0:T(8,128)}, f32[96,768]{1,0:T(8,128)}, f32[2,96,768]{2,1,0:T(8,128)}...) custom-call(bf16[256,768]{1,0:T(8,128)(2,1)} %refs_0_.3, ...), custom_call_target="tpu_custom_call" | custom-call | tf_op jit(solution)/shard_map/layers_backward/pallas_call | solution.py:1141
  345.5 0.0 copy-start
  345.5 12.2 %write_grads.1 = (f32[256,768]{1,0:T(8,128)}, f32[2,768]{1,0:T(2,128)}, f32[2,768]{1,0:T(2,128)}, f32[2,1536]{1,0:T(2,128)}, f32[2,768]{1,0:T(2,128)}, /*index=5...) custom-call(f32[256,768]{1,0:T(8,128)} %get-tuple-element.86.refs_0_, ...), custom_call_target="tpu_custom_call" | custom-call | tf_op jit(solution)/shard_map/write_grads/pallas_call | solution.py:1243
  357.7 0.0 copy-done
  357.7 0.7 copy.27
Async XLA Ops:
  345.5 12.3 %copy-start = (bf16[256,768]{1,0:T(8,128)(2,1)S(1)}, bf16[256,768]{1,0:T(8,128)(2,1)}, u32[]{:S(2)}) copy-start(bf16[256,768]{1,0:T(8,128)(2,1)} %get-tuple-element.116) | copy-start | bytes 1179652
where the time goes:
time: 364 us; the launch traced here: 359 us
  Pallas kernels  356 us (98%)
    pallas_call x1, Pallas kernels, forward(): pl.pallas_call(kernel, out_shape=out_shape, in_specs=[vmem_spec()] * len(...  174 us
    pallas_call x1, Pallas kernels, backward(): pl.pallas_call(kernel, out_shape=out_shape, in_specs=in_specs, out_specs=...  170 us
    pallas_call x1, Pallas kernels, finish(): pl.pallas_call(kernel, grid=(steps,), out_shape=[*[jax.ShapeDtypeStruct(e...  12.2 us

commit v1 on v0

--- a/solution.py
+++ b/solution.py
@@ -15,7 +15,6 @@
 EPS = 1e-05
 LIMIT = 60 << 20
 
-
 def norm(rows):
     centred = rows - jnp.mean(rows, axis=-1, keepdims=True)
     rstd = lax.rsqrt(jnp.mean(centred * centred, axis=-1, keepdims=True) + EPS)
@@ -67,82 +66,98 @@
     return pl.ds(pl.multiple_of(start, size), size)
 
 
-class Group:
-    def __init__(self, sems, ids, gathered, pair_out, pair_in, own_out, own_in, far_out, far_in):
-        self.sems = sems
-        self.ids = ids
-        self.gathered = gathered
-        self.pair_out, self.pair_in = pair_out, pair_in
-        self.own_out, self.own_in = own_out, own_in
-        self.far_out, self.far_in = far_out, far_in
-        self.half = gathered.shape[0] // 8
+class Gather:
+    def __init__(self, sems, ids, rows):
+        self.sems, self.ids, self.rows = sems, ids, rows
+        self.half = rows.shape[0] // 8
 
     def copy(self, src, dst, kind, part, far):
         send, recv = self.sems
         return pltpu.make_async_remote_copy(
-            src_ref=src,
-            dst_ref=dst,
+            src_ref=self.rows.at[span(src, self.half)],
+            dst_ref=self.rows.at[span(dst, self.half)],
             send_sem=send.at[kind, part],
             recv_sem=recv.at[kind, part],
             device_id=self.ids[1] if far else self.ids[0],
             device_id_type=MESH,
         )
 
-    def rows(self, start):
-        return pl.ds(pl.multiple_of(start, self.half), self.half)
+    def own(self, part):
+        return span(2 * self.half * part, self.half)
 
     def pair(self, part):
         return 6 * self.half - 2 * self.half * part
 
     def far_copy(self, part):
-        own = self.gathered.at[self.rows(part * self.half)]
-        return self.copy(own, self.gathered.at[self.rows(self.pair(part))], 0, part, True)
+        return self.copy(2 * self.half * part, self.pair(part), 0, part, True)
 
     def sibling_copy(self, part):
-        own = self.gathered.at[self.rows(part * self.half)]
-        place = self.gathered.at[self.rows((2 + part) * self.half)]
-        return self.copy(own, place, 1, part, False)
+        start = 2 * self.half * part
+        return self.copy(start, start + self.half, 1, part, False)
 
     def forward_copy(self, part):
-        src = self.gathered.at[self.rows(self.pair(part))]
-        dst = self.gathered.at[self.rows(self.pair(part) + self.half)]
-        return self.copy(src, dst, 2, part, False)
+        return self.copy(self.pair(part), self.pair(part) + self.half, 2, part, False)
 
     def send(self, part):
         self.far_copy(part).start()
         self.sibling_copy(part).start()
 
+    def near(self, part):
+        self.sibling_copy(part).wait_recv()
+
+    def far(self, part):
+        self.far_copy(part).wait_recv()
+        self.forward_copy(part).start()
+        self.forward_copy(part).wait()
+
     def receive(self, step):
-        @pl.when(step == 1)
+        @pl.when(step < 2)
         def _():
-            self.sibling_copy(0).wait_recv()
-            self.sibling_copy(1).wait_recv()
+            self.near(step)
 
         @pl.when(step >= 2)
         def _():
-            part = step - 2
-            self.far_copy(part).wait_recv()
-            self.forward_copy(part).start()
-            self.forward_copy(part).wait()
+            self.far(step - 2)
+
+    def finish(self, far=True):
+        for part in range(2):
+            self.sibling_copy(part).wait_send()
+            if far:
+                self.far_copy(part).wait_send()
+
+
+class Scatter:
+    def __init__(self, sems, ids, own, buffers):
+        self.sems, self.ids, self.own_sum = sems, ids, own
+        self.pair_out, self.pair_in, self.own_out, self.own_in, self.far_out, self.far_in = buffers
+        self.half = self.pair_out.shape[1]
+
+    def copy(self, src, dst, kind, part, far):
+        send, recv = self.sems
+        return pltpu.make_async_remote_copy(
+            src_ref=src.at[part],
+            dst_ref=dst.at[part],
+            send_sem=send.at[kind, part],
+            recv_sem=recv.at[kind, part],
+            device_id=self.ids[1] if far else self.ids[0],
+            device_id_type=MESH,
+        )
 
     def pair_copy(self, part):
-        return self.copy(self.pair_out.at[part], self.pair_in.at[part], 3, part, False)
-
-    def own_copy(self):
-        return self.copy(self.own_out, self.own_in, 4, 0, False)
+        return self.copy(self.pair_out, self.pair_in, 0, part, False)
+
+    def own_copy(self, part):
+        return self.copy(self.own_out, self.own_in, 1, part, False)
 
     def sum_copy(self, part):
-        return self.copy(self.far_out.at[part], self.far_in.at[part], 5, part, True)
-
-    def scatter(self, unit, total, own):
-        @pl.when(unit == 0)
+        return self.copy(self.far_out, self.far_in, 2, part, True)
+
+    def send(self, unit, total):
+        @pl.when(unit < 2)
         def _():
-            own[...] = total[...]
-
-        @pl.when(unit == 1)
-        def _():
-            self.own_out[...] = total[...].astype(BF)
-            self.own_copy().start()
+            self.own_sum[span(self.half * unit, self.half), :] = total[: self.half, :]
+            self.own_out[unit] = total[self.half :, :].astype(BF)
+            self.own_copy(unit).start()
 
         @pl.when(unit >= 2)
         def _():
@@ -155,20 +170,103 @@
             ).astype(BF)
             self.sum_copy(part).start()
 
-    def collect(self, part, own):
-        if part == 0:
-            self.own_copy().wait_recv()
+    def collect(self, part):
+        self.own_copy(part).wait_recv()
         self.sum_copy(part).wait_recv()
         rows = pl.ds(part * self.half, self.half)
-        return own[rows, :] + self.own_in[rows, :].astype(F32) + self.far_in[part].astype(F32)
+        made = self.own_sum[rows, :] + self.own_in[part].astype(F32)
+        return made + self.far_in[part].astype(F32)
 
     def finish(self):
         for part in range(2):
-            self.far_copy(part).wait_send()
-            self.sibling_copy(part).wait_send()
             self.pair_copy(part).wait_send()
+            self.own_copy(part).wait_send()
             self.sum_copy(part).wait_send()
-        self.own_copy().wait_send()
+
+
+class Near:
+    def __init__(self, sems, ids, own, out, into):
+        self.sems, self.ids = sems, ids
+        self.own, self.out, self.into = own, out, into
+        self.half = out.shape[1]
+
+    def copy(self, part):
+        return pltpu.make_async_remote_copy(
+            src_ref=self.out.at[part],
+            dst_ref=self.into.at[part],
+            send_sem=self.sems.at[0, part],
+            recv_sem=self.sems.at[1, part],
+            device_id=self.ids[0],
+            device_id_type=MESH,
+        )
+
+    def send(self, part, total):
+        self.own[span(self.half * part, self.half), :] = total[: self.half, :]
+        self.out[part] = total[self.half :, :].astype(BF)
+        self.copy(part).start()
+
+    def collect(self, part):
+        self.copy(part).wait_recv()
+        return self.own[pl.ds(part * self.half, self.half), :] + self.into[part].astype(F32)
+
+    def drain(self):
+        for part in range(2):
+            self.copy(part).wait_send()
+
+
+class Fetch:
+    def __init__(self, sems, ids, square, shards):
+        self.sems, self.shards = sems, shards
+        self.far = ids[1]
+        self.x, self.z, self.x_peer, self.z_peer = square
+        self.piece = shards.shape[1] // 8
+
+    def copy(self, index, src, start, size, device):
+        place = span(start * self.piece, size * self.piece)
+        return pltpu.make_async_remote_copy(
+            src_ref=self.shards.at[src, place],
+            dst_ref=self.shards.at[1, place],
+            send_sem=self.sems.at[0, index],
+            recv_sem=self.sems.at[1, index],
+            device_id=device,
+            device_id_type=MESH,
+        )
+
+    def hop(self, index):
+        x_first = 2 * self.z + self.x
+        z_first = 4 + 2 * self.x + self.z
+        return (
+            lambda: self.copy(0, 0, x_first, 1, self.far),
+            lambda: self.copy(1, 0, z_first, 1, self.far),
+            lambda: self.copy(2, 1, x_first, 1, self.x_peer),
+            lambda: self.copy(3, 1, z_first, 1, self.z_peer),
+            lambda: self.copy(4, 1, 2 * self.z, 2, self.z_peer),
+            lambda: self.copy(5, 1, 4 + 2 * self.x, 2, self.x_peer),
+        )[index]()
+
+    def step(self, count):
+        if count == 1:
+            self.hop(0).start()
+            self.hop(1).start()
+        elif count < 4:
+            for index in (2 * count - 4, 2 * count - 3):
+                self.hop(index).wait_recv()
+                self.hop(index + 2).start()
+        else:
+            self.hop(4).wait_recv()
+            self.hop(5).wait_recv()
+
+    def finish(self):
+        for index in range(6):
+            self.hop(index).wait_send()
+
+
+def square():
+    group = lax.axis_index("dp")
+    place = lax.axis_index("tensor")
+    x = lax.rem(group, 2)
+    z = lax.rem(group // 2, 2)
+    return (x, z, (group + 1 - 2 * x, place), (group + 2 - 4 * z, place))
 
 
 def neighbours():
@@ -273,17 +371,8 @@
             self.z_copy(ahead).wait_send()
 
 
-def group_scratch(rows, width):
-    half = rows // 8
-    return [
-        pltpu.VMEM((rows, width), BF),
-        pltpu.VMEM((2, half, width), BF),
-        pltpu.VMEM((2, half, width), BF),
-        pltpu.VMEM((2 * half, width), BF),
-        pltpu.VMEM((2 * half, width), BF),
-        pltpu.VMEM((2, half, width), BF),
-        pltpu.VMEM((2, half, width), BF),
-    ]
+def scatter_scratch(rows, width):
+    return [pltpu.VMEM((2, rows // 8, width), BF)] * 6
 
 
 def gelu_parts(hidden):
@@ -303,7 +392,7 @@
 
 
 def owner(chunk):
-    return jnp.where(chunk < 4, chunk // 2, 2 + chunk % 2)
+    return 2 * (chunk // 4) + chunk % 2
 
 
 def apart(keys, queries, packed):
@@ -311,7 +400,7 @@
 
 
 def unit_owner(unit, half):
-    return jnp.where(unit < 2, unit, 2 + half)
+    return jnp.where(unit < 2, 0, 2) + half
 
 
 SAVED = ("a", "q", "k", "v", "o", "x1", "m", "g", "slope", "x", "lse")
@@ -326,23 +415,34 @@
         return made
 
     (gain_ref, bias_ref, bdown_ref, bada_ref, lengths_ref, steps_ref) = take(6)
-    (rotary_ref, time_ref) = take(2)
+    (rotary_ref, time_ref, cot_ref) = take(3)
     (tokens_hbm, wself_hbm, wqkv_hbm, wout_hbm, wup_hbm, wdown_hbm, wada_hbm) = take(7)
-    (acts_ref, est_ref, cond_ref, cos_ref, sin_ref, temb_ref) = take(6)
+    (acts_ref, est_ref, cond_ref, cos_ref, sin_ref, temb_ref, grad_hbm) = take(7)
     saved_hbm = [dict(zip(SAVED, take(len(SAVED)))) for _ in range(depth)]
-    (send, recv, send2, recv2, load_sems, store_sems) = take(6)
+    gather_sems = [take(2) for _ in range(5)]
+    (near_a_sems, near_f_sems, fetch_sems, cross_send, cross_recv) = take(5)
+    (load_sems, store_sems) = take(2)
     (tokens, wself, wada) = take(3)
-    weights = [take(6) for _ in range(depth)]
-    wqks = take(depth)
-    first, second = take(7), take(7)
-    (qb, kb, vb, lse, ob, x1, gb, gpb, total, own, xb, start) = take(12)
+    wa, wu, wd, wqk = take(depth), take(depth), take(depth), take(depth)
+    abufs, mbufs, (ebuf,) = take(2), take(2), take(1)
+    (q2, k2, v2, ob2, lse2, accs, stats, gb, gpb) = take(9)
+    (x1, xb, start, own_a, own_f, sums) = take(6)
+    near_a_bufs, near_f_bufs = take(2), take(2)
     ids = neighbours()
+    corner = square()
+    columns = heads * HD
+    width = xb.shape[1]
+    half = xb.shape[0] // 2
+    unit_rows = 2 * half
+    length = 8 * half
+    part_a = [pl.ds(part * columns, columns) for part in range(4)]
     sources = [tokens_hbm, wself_hbm.at[0], wself_hbm.at[1]]
     places = [tokens, wself.at[0], wself.at[1]]
     for layer in range(depth):
-        sources += [wqkv_hbm.at[layer, part] for part in range(3)]
-        sources += [wout_hbm.at[layer], wup_hbm.at[layer], wdown_hbm.at[layer]]
-        places += weights[layer]
+        sources += [wqkv_hbm.at[layer, part] for part in range(3)] + [wout_hbm.at[layer]]
+        places += [wa[layer].at[0, rows] for rows in part_a]
+        sources += [wup_hbm.at[layer], wdown_hbm.at[layer]]
+        places += [wu[layer].at[0], wd[layer].at[0]]
     loads = [
         pltpu.make_async_copy(src, dst, load_sems.at[i])
         for i, (src, dst) in enumerate(zip(sources, places))
@@ -358,47 +458,52 @@
     for i in range(len(loads)):
         if i not in order:
             loads[i].start()
-    meet(ids)
-    attn = Group((send, recv), ids, *first)
-    feed = Group((send2, recv2), ids, *second)
-    abuf, mbuf = first[0], second[0]
-    half = attn.half
-    unit_rows = 2 * half
-    length = 8 * half
-    width = xb.shape[1]
-    columns = heads * HD
+    meet([*ids, *corner[2:]])
+    fetches = []
+    for layer in range(depth):
+        for shards in (wa[layer], wu[layer], wd[layer]):
+            fetches.append(Fetch(fetch_sems.at[len(fetches)], ids, corner, shards))
+    gathers = [Gather(gather_sems[i], ids, abufs[i]) for i in range(2)]
+    mixes = [Gather(gather_sems[2 + i], ids, mbufs[i]) for i in range(2)]
+    grads = Gather(gather_sems[4], ids, ebuf)
+    near_a = Near(near_a_sems, ids, own_a, *near_a_bufs)
+    near_f = Near(near_f_sems, ids, own_f, *near_f_bufs)
     packed = is_packed(lengths_ref, length)
-    buffers = dict(zip(SAVED, (abuf, qb, kb, vb, ob, x1, mbuf, gb, gpb, xb, lse)))
     pending = []
 
-    def store(layer, *names):
-        for name in names:
-            made = pltpu.make_async_copy(
-                buffers[name], saved_hbm[layer][name], store_sems.at[SAVED.index(name)]
-            )
-            made.start()
-            pending.append((name, made))
+    def store(name, src, dst):
+        made = pltpu.make_async_copy(src, dst, store_sems.at[len(pending)])
+        made.start()
+        pending.append([name, made, False])
 
     def stored(*names):
-        for each in list(pending):
-            if each[0] in names:
+        for each in pending:
+            if each[0] in names and not each[2]:
                 each[1].wait()
-                pending.remove(each)
-
-    def begin(layer, part, rows, values):
-        xb[rows, :] = values
-        hat = norm(values)[0]
+                each[2] = True
+
+    def begin(number, part, made):
+        layer = number % depth
+        rows = pl.ds(part * half, half)
+        if number >= 2 and part == 0:
+            gathers[number % 2].finish()
+        xb[rows, :] = made
+        hat = norm(made)[0]
         gain = gain_ref[layer : layer + 1, :]
-        abuf[rows, :] = (hat * gain + bias_ref[layer : layer + 1, :]).astype(BF)
-        attn.send(part)
-
+        normed = hat * gain + bias_ref[layer : layer + 1, :]
+        abufs[number % 2][pl.ds(2 * half * part, half), :] = normed.astype(BF)
+        gathers[number % 2].send(part)
+
+    for i in (3, 4, 5, 6):
+        loads[i].wait()
+    fetches[0].step(1)
     loads[0].wait()
     loads[1].wait()
     for part in range(2):
         rows = pl.ds(part * half, half)
         made = dot(tokens[rows, :], wself[0])
         start[rows, :] = made
-        begin(0, part, rows, made)
+        begin(0, part, made)
 
     def make_tables():
         place = lax.axis_index("tensor")
@@ -408,8 +513,8 @@
         row = lax.broadcasted_iota(jnp.int32, (half, 128), 0).astype(F32)
         for chunk, (block, part) in enumerate(
             zip(
-                (place, place, sibling, sibling, far, far_other, far, far_other),
-                (0, 1, 0, 1, 1, 1, 0, 0),
+                (place, sibling, place, sibling, far, far_other, far, far_other),
+                (0, 0, 1, 1, 1, 1, 0, 0),
             )
         ):
             rows = pl.ds(chunk * half, half)
@@ -435,132 +540,375 @@
         if layer + 1 < depth:
             ada_loads[layer + 1].start()
 
-    def run(layer, save, after_layer):
-        (wq, wk, wv, wout, wup, wdown) = weights[layer]
-        wqk = wqks[layer]
-        if not save:
+    def project(number, count, pick, before):
+        layer = number % depth
+        abuf = abufs[number % 2]
+
+        def body(step, carry):
+            before(step)
+            shard, unit = pick(step)
+            rows = span(unit * unit_rows, unit_rows)
+            normed = abuf[rows, :]
+            mixed = dot(normed, wqk[layer][shard], NT)
+            cosine = cos_ref[rows, :]
+            sine = sin_ref[rows, :]
+            for place, dst, scale in ((0, q2, HD**-0.5), (256, k2, 1.0)):
+                first = mixed[:, place : place + 128]
+                second = mixed[:, place + 128 : place + 256]
+                dst[shard, rows, :128] = ((first * cosine - second * sine) * scale).astype(BF)
+                dst[shard, rows, 128:] = ((second * cosine + first * sine) * scale).astype(BF)
+            v2[shard, rows, :] = dot(normed, wa[layer][shard, part_a[2], :], NT).astype(BF)
+            return carry
+
+        lax.fori_loop(0, count, body, 0)
+
+    lane = lax.broadcasted_iota(jnp.int32, (1, 128), 1)
+
+    def scores_of(shard, unit, head, keys):
+        rows = span(unit * unit_rows, unit_rows)
+        made = dot(keep_head(q2[shard, rows, :], head, True), k2[shard, keys, :], NT)
+        part = lax.broadcasted_iota(jnp.int32, (2, 1, length // 2), 0)
+        chunk = lax.broadcasted_iota(jnp.int32, (2, 1, length // 2), 2) // half
+        neg = apart(owner(chunk + keys.start // half), part, packed.reshape(1, 1, 1))
+        return (made.reshape(2, half, length // 2) + neg).reshape(unit_rows, length // 2)
+
+    def attend_near(number, count, pick, before):
+        keys = pl.ds(0, length // 2)
+
+        def body(step, carry):
+            before(step)
+            shard, unit = pick(step)
+            place = 2 * unit + shard
+            attended = jnp.zeros((unit_rows, columns), F32)
+            tops = jnp.zeros((unit_rows, 128), F32)
+            totals = jnp.zeros((unit_rows, 128), F32)
+            for head in range(heads):
+                scores = scores_of(shard, unit, head, keys)
+                largest = jnp.max(scores, axis=-1, keepdims=True)
+                shares = jnp.exp(scores - largest)
+                output = dot(shares.astype(BF), v2[shard, keys, :])
+                attended = jnp.where(head_mask(head, columns, False), output, attended)
+                tops = jnp.where(lane == head, largest, tops)
+                totals = jnp.where(lane == head, jnp.sum(shares, axis=-1, keepdims=True), totals)
+            accs[place] = attended
+            stats[place, 0] = tops
+            stats[place, 1] = totals
+            return carry
+
+        lax.fori_loop(0, count, body, 0)
+
+    def attend_far(number, save, before):
+        keys = pl.ds(length // 2, length // 2)
+        layer, slot = number % depth, number % 2
+
+        def body(step, carry):
+            before(step)
+            shard, unit = by_unit(step)
+            place = 2 * unit + shard
+            rows = span(unit * unit_rows, unit_rows)
+            attended = jnp.zeros((unit_rows, columns), F32)
+            logs = jnp.zeros((unit_rows, 128), F32)
+            for head in range(heads):
+                scores = scores_of(shard, unit, head, keys)
+                earlier = stats[place, 0][:, head : head + 1]
+                largest = jnp.maximum(earlier, jnp.max(scores, axis=-1, keepdims=True))
+                shares = jnp.exp(scores - largest)
+                shrink = jnp.exp(earlier - largest)
+                totals = stats[place, 1][:, head : head + 1] * shrink
+                totals = totals + jnp.sum(shares, axis=-1, keepdims=True)
+                output = dot(shares.astype(BF), v2[shard, keys, :])
+                output = (accs[place] * shrink + output) * (1.0 / totals)
+                attended = jnp.where(head_mask(head, columns, False), output, attended)
+                if save:
+                    logs = jnp.where(lane == head, largest + jnp.log(totals), logs)
+            if save:
+                lse2[slot, shard, unit] = logs.T[:8, :]
+            attended = attended.astype(BF)
+            ob2[slot, shard, rows, :] = attended
+
+            @pl.when(shard == 1)
+            def _():
+                total = dot(ob2[slot, 0, rows, :], wa[layer][0, part_a[3], :])
+                near_a.send(unit, total + dot(attended, wa[layer][1, part_a[3], :]))
+
+            return carry
+
+        lax.fori_loop(0, 4, body, 0)
+
+    def feed(number, save, pick, before):
+        layer = number % depth
+        mbuf = mbufs[number % 2]
+
+        def body(step, carry):
+            before(step)
+            shard, unit = pick(step)
+            rows = span(unit * unit_rows, unit_rows)
+            hidden = dot(mbuf[rows, :], wu[layer][shard])
+            gated, slope = gelu_parts(hidden)
+            gated = gated.astype(BF)
+            made = dot(gated, wd[layer][shard])
+
+            @pl.when(shard == 0)
+            def _():
+                if save:
+                    gb[rows, :] = gated
+                    gpb[rows, :] = slope.astype(BF)
+                sums[rows, :] = made
+
+            @pl.when(shard == 1)
+            def _():
+                near_f.send(unit, sums[rows, :] + made)
+
+            return carry
+
+        lax.fori_loop(0, 4, body, 0)
+
+    crossings = {}
+
+    def cross(number):
+        slot = number % 2
+        made = []
+        for part in range(2):
+            pairs = (
+                (
+                    ob2.at[slot, 1, pl.ds(part * unit_rows, unit_rows)],
+                    ob2.at[slot, 0, pl.ds((3 - part) * unit_rows, unit_rows)],
+                ),
+                (lse2.at[slot, 1, part], lse2.at[slot, 0, 3 - part]),
+            )
+            for kind, (src, dst) in enumerate(pairs):
+                place = 4 * slot + 2 * part + kind
+                made.append(
+                    pltpu.make_async_remote_copy(
+                        src_ref=src,
+                        dst_ref=dst,
+                        send_sem=cross_send.at[place],
+                        recv_sem=cross_recv.at[place],
+                        device_id=ids[1],
+                        device_id_type=MESH,
+                    )
+                )
+                made[-1].start()
+        crossings[number] = made
+
+    def late(number):
+        slot = number % 2
+        saved = saved_hbm[number % depth]
+        if number == depth:
+            for part in range(2):
+                grads.near(part)
+                grads.far(part)
+            store("grad", ebuf, grad_hbm)
+        for part in range(2):
+            mixes[slot].far(part)
+        store("m", mbufs[slot], saved["m"])
+        for each in crossings[number]:
+            each.wait_recv()
+        store("o", ob2.at[slot, 0], saved["o"])
+        store("lse", lse2.at[slot, 0], saved["lse"])
+
+    def steps_of(*pairs):
+        for index, count in pairs:
+            if index < len(fetches):
+                fetches[index].step(count)
+
+    def events(table):
+        def before(step):
+            for when, actions in table.items():
+
+                @pl.when(step == when)
+                def _():
+                    for action in actions:
+                        if isinstance(action, tuple):
+                            if action[0] < len(fetches):
+                                fetches[action[0]].step(action[1])
+                        else:
+                            action()
+
+        return before
+
+    def waits(*indices):
+        def action():
+            for index in indices:
+                loads[index].wait()
+
+        return action
+
+    def by_unit(step):
+        return (lax.rem(step, 2), step // 2)
+
+    def by_shard(step):
+        return (step // 2, lax.rem(step, 2))
+
+    def run(number, after_layer):
+        layer, slot = number % depth, number % 2
+        save = number >= depth
+        group, mix = gathers[slot], mixes[slot]
+        mix_rows = mbufs[slot]
+        base = 3 * layer
+
+        def after_attend(part):
+            def action():
+                if part == 0 and number >= 2:
+                    mix.finish(far=False)
+                if part == 0:
+                    stored("x1")
+                rows = pl.ds(part * half, half)
+                after = xb[rows, :] + near_a.collect(part)
+                x1[rows, :] = after
+                shift = cond_ref[8 * layer : 8 * layer + 1, :width]
+                scale = cond_ref[8 * layer : 8 * layer + 1, width:]
+                made = norm(after)[0] * (1.0 + scale) + shift
+                mix_rows[pl.ds(2 * half * part, half), :] = made.astype(BF)
+                mix.sibling_copy(part).start()
+                if save:
+                    mix.far_copy(part).start()
+
+            return action
+
+        def after_feed(part):
+            def action():
+                if part == 0:
+                    stored("x")
+                rows = pl.ds(part * half, half)
+                made = x1[rows, :] + near_f.collect(part) + bdown_ref[layer : layer + 1, :]
+                after_layer(part, rows, made)
+
+            return action
+
+        def near_rows(part):
+            return lambda: group.near(part)
+
+        def far_rows(part):
+            return lambda: group.far(part)
+
+        def mixed(part):
+            return lambda: mix.near(part)
+
+        if number:
+            near_a.drain()
+            near_f.drain()
+        stored("q", "k", "v")
+        if save:
+            if number == depth:
+                for part in range(2):
+                    ebuf[grads.own(part), :] = cot_ref[pl.ds(part * half, half), :]
+                    grads.send(part)
+            arrive = events({0: [near_rows(0)], 1: [near_rows(1)]})
+            project(number, 4, by_shard, arrive)
+            attend_near(number, 4, by_unit, events({}))
+            if number > depth:
+                late(number - 1)
+            arrive = events({0: [far_rows(0)], 2: [far_rows(1)]})
+            project(number, 4, lambda step: (lax.rem(step, 2), 3 - step // 2), arrive)
+            store("a", abufs[slot], saved_hbm[layer]["a"])
+            store("x", xb, saved_hbm[layer]["x"])
+            for name, src in (("q", q2), ("k", k2), ("v", v2)):
+                store(name, src.at[0], saved_hbm[layer][name])
+            far_table = {3: [after_attend(0)]}
+            feed_table = {
+                0: [mixed(0)],
+                1: [after_attend(1)],
+                2: [mixed(1)],
+                3: [after_feed(0)],
+            }
+            order = by_unit
+        else:
             if layer == 0:
                 make_tables()
-            for i in range(3 + 6 * layer, 6 + 6 * layer):
-                loads[i].wait()
-            load_turned(wq, wk, wqk)
-        stored("q", "k", "v")
-
-        def project(step, carry):
-            attn.receive(step)
-            unit = jnp.where(step < 2, step, 5 - step)
-            rows = span(unit * unit_rows, unit_rows)
-            normed = abuf[rows, :]
-            mixed = dot(normed, wqk[...], NT)
-            cosine = cos_ref[rows, :]
-            sine = sin_ref[rows, :]
-            for place, dst, scale in ((0, qb, HD**-0.5), (256, kb, 1.0)):
-                first_half = mixed[:, place : place + 128]
-                second_half = mixed[:, place + 128 : place + 256]
-                dst[rows, :128] = ((first_half * cosine - second_half * sine) * scale).astype(BF)
-                dst[rows, 128:] = ((second_half * cosine + first_half * sine) * scale).astype(BF)
-            vb[rows, :] = dot(normed, wv[...], NT).astype(BF)
-            return carry
-
-        lax.fori_loop(0, 4, project, 0)
-        stored("o", "lse", "m", "x1", "g", "slope")
+            load_turned(
+                wa[layer].at[0, part_a[0]], wa[layer].at[0, part_a[1]], wqk[layer].at[0]
+            )
+            rows_table = {
+                0: [near_rows(0)],
+                1: [near_rows(1)],
+                2: [far_rows(0)],
+                3: [far_rows(1)],
+            }
+            if layer == 0:
+                rows_table[2] = [(0, 2), far_rows(0)]
+                rows_table[3] = [far_rows(1), waits(7), (1, 1)]
+                first_near = {0: [(0, 3)]}
+                second_near = {1: [(1, 3)]}
+                far_table = {0: [(2, 2), waits(9, 10, 11, 12), (3, 1)], 3: [after_attend(0)]}
+                feed_table = {
+                    0: [mixed(0), (3, 2), waits(13), (4, 1)],
+                    1: [after_attend(1), mixed(1), (2, 3), (1, 4)],
+                    2: [(2, 4), (3, 3), (4, 2), waits(14), (5, 1)],
+                    3: [after_feed(0)],
+                }
+                order = by_shard
+            else:
+                rows_table[2] = [(base + 1, 3), *rows_table[2]]
+                rows_table[3] = [*rows_table[3], (base + 2, 2)]
+                first_near = {}
+                second_near = {0: [(base + 2, 3)]}
+                far_table = {3: [after_attend(0)]}
+                feed_table = {
+                    0: [mixed(0), (base + 1, 4)],
+                    1: [after_attend(1), (base + 2, 4)],
+                    2: [mixed(1)],
+                    3: [after_feed(0)],
+                }
+                order = by_unit
+
+            def in_order(step):
+                return jnp.where(step < 2, step, 5 - step)
+
+            project(number, 4, lambda step: (0, in_order(step)), events(rows_table))
+            attend_near(number, 2, lambda step: (0, step), events(first_near))
+            make_cond(layer)
+            if layer == 0:
+                events({0: [waits(8), (2, 1), (1, 2)]})(0)
+            events({0: [(base, 4)]})(0)
+            load_turned(
+                wa[layer].at[1, part_a[0]], wa[layer].at[1, part_a[1]], wqk[layer].at[1]
+            )
+            project(number, 4, lambda step: (1, in_order(step)), events({}))
+            attend_near(number, 2, lambda step: (1, step), events(second_near))
+        attend_far(number, save, events(far_table))
         if save:
-            store(layer, "a", "x", "q", "k", "v")
-        elif layer == 0:
-            for i in (6, 7, 8):
-                loads[i].wait()
-        else:
-            for i in range(6 + 6 * layer, 9 + 6 * layer):
-                loads[i].wait()
-        lane = lax.broadcasted_iota(jnp.int32, (1, 128), 1)
-
-        def attend(step, carry):
-            unit = 3 - step
-            rows = span(unit * unit_rows, unit_rows)
-            queries = qb[rows, :]
-            attended = jnp.zeros((unit_rows, columns), F32)
-            logs = jnp.zeros((unit_rows, 128), F32)
-            part = lax.broadcasted_iota(jnp.int32, (2, 1, length), 0)
-            chunk = lax.broadcasted_iota(jnp.int32, (2, 1, length), 2) // half
-            neg = apart(owner(chunk), unit_owner(unit, part), packed.reshape(1, 1, 1))
-            for head in range(heads):
-                scores = dot(keep_head(queries, head, True), kb[...], NT)
-                scores = scores.reshape(2, half, length) + neg
-                scores = scores.reshape(unit_rows, length)
-                largest = jnp.max(scores, axis=-1, keepdims=True)
-                shares = jnp.exp(scores - largest)
-                sums = jnp.sum(shares, axis=-1, keepdims=True)
-                output = dot(shares.astype(BF), vb[...]) * (1.0 / sums)
-                attended = jnp.where(head_mask(head, columns, False), output, attended)
-                if save:
-                    logs = jnp.where(lane == head, largest + jnp.log(sums), logs)
-            if save:
-                lse[unit] = logs.T[:8, :]
-            attended = attended.astype(BF)
-            ob[rows, :] = attended
-            total[...] = dot(attended, wout[...])
-            attn.scatter(unit, total, own)
-            return carry
-
-        lax.fori_loop(0, 4, attend, 0)
-        if not save:
-            make_cond(layer)
-        shift = cond_ref[8 * layer : 8 * layer + 1, :width]
-        scale = cond_ref[8 * layer : 8 * layer + 1, width:]
-        if save or layer:
-            feed.finish()
-        for part in range(2):
-            rows = pl.ds(part * half, half)
-            after = xb[rows, :] + attn.collect(part, own)
-            x1[rows, :] = after
-            mbuf[rows, :] = (norm(after)[0] * (1.0 + scale) + shift).astype(BF)
-            feed.send(part)
-        stored("a", "x")
+            cross(number)
+        stored("g", "slope")
+        feed(number, save, order, events(feed_table))
         if save:
-            store(layer, "o", "lse", "x1")
-
-        def expand(step, carry):
-            feed.receive(step)
-            unit = jnp.where(step < 2, step, 5 - step)
-            rows = span(unit * unit_rows, unit_rows)
-            hidden = dot(mbuf[rows, :], wup[...])
-            gated, slope = gelu_parts(hidden)
-            gated = gated.astype(BF)
-            if save:
-                gb[rows, :] = gated
-                gpb[rows, :] = slope.astype(BF)
-            total[...] = dot(gated, wdown[...])
-            feed.scatter(unit, total, own)
-            return carry
-
-        lax.fori_loop(0, 4, expand, 0)
-        if save:
-            store(layer, "m", "g", "slope")
-        attn.finish()
-        for part in range(2):
-            rows = pl.ds(part * half, half)
-            made = x1[rows, :] + feed.collect(part, own) + bdown_ref[layer : layer + 1, :]
-            after_layer(part, rows, made)
+            store("x1", x1, saved_hbm[layer]["x1"])
+            store("g", gb, saved_hbm[layer]["g"])
+            store("slope", gpb, saved_hbm[layer]["slope"])
+        after_feed(1)()
 
     def between(part, rows, made):
         estimate = made.astype(BF)
         est_ref[rows, :] = estimate
-        begin(0, part, rows, start[rows, :] + dot(estimate, wself[1]))
+        begin(depth, part, start[rows, :] + dot(estimate, wself[1]))
 
     def close(part, rows, made):
         acts_ref[rows, :] = made.astype(BF)
 
-    for save in (False, True):
-        for layer in range(depth):
-            if layer + 1 < depth:
-                run(layer, save, functools.partial(begin, layer + 1))
-            elif save:
-                run(layer, save, close)
-            else:
-                loads[2].wait()
-                run(layer, save, between)
-    feed.finish()
-    stored(*SAVED)
+    def enter(number):
+        return lambda part, rows, made: begin(number, part, made)
+
+    for number in range(2 * depth):
+        if number + 1 == 2 * depth:
+            run(number, close)
+        elif number + 1 == depth:
+            loads[2].wait()
+            run(number, between)
+        else:
+            run(number, enter(number + 1))
+    late(2 * depth - 1)
+    for each in gathers:
+        each.finish()
+    for each in (*mixes, grads):
+        each.finish()
+    near_a.drain()
+    near_f.drain()
+    for each in fetches:
+        each.finish()
+    for each in crossings.values():
+        for copy in each:
+            copy.wait_send()
+    stored("grad", *SAVED)
 
 
 def any_spec():
@@ -571,10 +919,11 @@
     return pl.BlockSpec(memory_space=pltpu.VMEM)
 
 
-def forward(heads, tokens, w_self, vectors, weights):
+def forward(heads, tokens, cotangent, w_self, vectors, weights):
     depth = weights[0].shape[0]
     block, width = tokens.shape
     length = 4 * block
+    half = block // 2
     columns = heads * HD
     units = weights[2].shape[2]
     lanes = jnp.arange(128) % HALF
@@ -589,8 +938,8 @@
         "o": ((length, columns), BF),
         "x1": ((block, width), F32),
         "m": ((length, width), BF),
-        "g": ((length, units), BF),
-        "slope": ((length, units), BF),
+        "g": ((length // 2, units), BF),
+        "slope": ((length // 2, units), BF),
         "x": ((block, width), F32),
         "lse": ((4, 8, block), F32),
     }
@@ -602,29 +951,42 @@
         jax.ShapeDtypeStruct((length, 128), F32),
         jax.ShapeDtypeStruct((length, 128), F32),
         jax.ShapeDtypeStruct((8, width), F32),
+        jax.ShapeDtypeStruct((length, width), BF),
     ] + kept_shapes * depth
-    out_specs = [vmem_spec()] * 6 + [any_spec()] * (depth * len(SAVED))
-    scratch = [pltpu.SemaphoreType.DMA((6, 2))] * 4
+    out_specs = [vmem_spec()] * 6 + [any_spec()] * (1 + depth * len(SAVED))
+    dma = pltpu.SemaphoreType.DMA
+    scratch = [dma((3, 2))] * 10
+    scratch += [dma((2, 2))] * 2 + [dma((3 * depth, 2, 6)), dma((8,)), dma((8,))]
+    scratch += [dma((4 + 6 * depth,)), dma((1 + depth * len(SAVED),))]
     scratch += [
-        pltpu.SemaphoreType.DMA((4 + 6 * depth,)),
-        pltpu.SemaphoreType.DMA((len(SAVED),)),
         pltpu.VMEM((block, width), BF),
         pltpu.VMEM((2, width, width), BF),
         pltpu.VMEM((width, 2 * width), F32),
     ]
-    for _ in range(depth):
-        scratch += [pltpu.VMEM((columns, width), BF)] * 3
-        scratch += [pltpu.VMEM(each.shape[1:], BF) for each in weights[1:4]]
-    scratch += [pltpu.VMEM((512, width), BF)] * depth
-    scratch += group_scratch(length, width) + group_scratch(length, width)
-    for name in ("q", "k", "v", "lse", "o", "x1", "g", "slope"):
-        scratch.append(pltpu.VMEM(*kept[name]))
-    scratch += [pltpu.VMEM((block, width), F32)] * 4
+    scratch += [pltpu.VMEM((2, 4 * columns, width), BF)] * depth
+    scratch += [pltpu.VMEM((2, width, units), BF)] * depth
+    scratch += [pltpu.VMEM((2, units, width), BF)] * depth
+    scratch += [pltpu.VMEM((2, 512, width), BF)] * depth
+    scratch += [pltpu.VMEM((length, width), BF)] * 5
+    scratch += [
+        pltpu.VMEM((2, length, 256), BF),
+        pltpu.VMEM((2, length, 256), BF),
+        pltpu.VMEM((2, length, columns), BF),
+        pltpu.VMEM((2, 2, length, columns), BF),
+        pltpu.VMEM((2, 2, 4, 8, block), F32),
+        pltpu.VMEM((4, block, columns), F32),
+        pltpu.VMEM((4, 2, block, 128), F32),
+        pltpu.VMEM((length // 2, units), BF),
+        pltpu.VMEM((length // 2, units), BF),
+    ]
+    scratch += [pltpu.VMEM((block, width), F32)] * 5
+    scratch += [pltpu.VMEM((2 * block, width), F32)]
+    scratch += [pltpu.VMEM((2, half, width), BF)] * 4
 
     def kernel(*refs):
         forward_kernel(depth, heads, refs)
 
-    operands = [*vectors, rotary, times]
+    operands = [*vectors, rotary, times, cotangent]
     remote = [tokens, w_self.reshape(2, width, width), *weights]
     made = pl.pallas_call(
         kernel,
@@ -638,8 +1000,8 @@
         name="layers_forward",
     )(*operands, *remote)
     count = len(SAVED)
-    saved = [made[6 + count * layer : 6 + count * (layer + 1)] for layer in range(depth)]
-    return (made[:6], [dict(zip(SAVED, each)) for each in saved])
+    saved = [made[7 + count * layer : 7 + count * (layer + 1)] for layer in range(depth)]
+    return (made[:7], [dict(zip(SAVED, each)) for each in saved])
 
 
 class Ladder:
@@ -704,13 +1066,15 @@
 
     cot_ref, gain_ref, lengths_ref, cos_ref, sin_ref, temb_ref, cond_ref = take(7)
     joined_hbm = take(2)
+    (grad_hbm,) = take(1)
     wqkv_hbm, wout_hbm, wup_hbm, wdown_hbm, _ = take(5)
     saved_hbm = [dict(zip(SAVED, take(len(SAVED)))) for _ in range(depth)]
     (out_ref, small_ref) = take(2)
     attn_outs, feed_outs = take(depth), take(depth)
     if deep:
         sum_ref, vec_ref = take(2)
-    send, recv, send2, recv2, load_sems, store_sems = take(6)
+    feed_sems, attn_sems = [take(2), take(2)], [take(2), take(2)]
+    load_sems, store_sems = take(2)
     loads = Loads(load_sems)
     wq, wk, wv = (
         loads.add(name, [wqkv_hbm.at[layer, part] for layer in range(depth)], take(1)[0])
@@ -720,12 +1084,16 @@
         loads.add(name, [src.at[layer] for layer in range(depth)], take(1)[0])
         for name, src in (("wout", wout_hbm), ("wup", wup_hbm), ("wdown", wdown_hbm))
     )
-    abuf, qb, kb, vb, ob, x1b, mbuf, gb, gpb, xb, lse = (
-        loads.add(name, [saved_hbm[layer][name] for layer in range(depth)], take(1)[0])
-        for name in SAVED
-    )
-    first = take(7)
-    second = take(7)
+    buffers = dict(zip(SAVED, take(len(SAVED))))
+    for name in SAVED:
+        rows = saved_hbm[0][name].shape[0]
+        buffer = buffers[name]
+        if rows < buffer.shape[0]:
+            buffer = buffer.at[pl.ds(0, rows)]
+        loads.add(name, [saved_hbm[layer][name] for layer in range(depth)], buffer)
+    abuf, qb, kb, vb, ob, x1b, mbuf, gb, gpb, xb, lse = (buffers[name] for name in SAVED)
+    ebuf, fbuf = take(2)
+    feed_bufs, attn_bufs = take(6), take(6)
     (wqk, dhb, qmask, domask, dsb, pb, dkb, dvb, dqk, dvv, work, dxb) = take(12)
     (feed_grads, attn_grads) = take(2)
     ids = neighbours()
@@ -750,22 +1118,20 @@
             each.start()
     else:
         meet(ids)
-    feed = Group((send, recv), ids, *first)
-    attn = Group((send2, recv2), ids, *second)
-    ebuf, fbuf = first[0], second[0]
-    half = feed.half
+    width = cot_ref.shape[1]
+    half = cot_ref.shape[0] // 2
     unit_rows = 2 * half
-    width = cot_ref.shape[1]
+    total, own, dx1 = (work.at[pl.ds(i * unit_rows, unit_rows)] for i in range(3))
+    feed_rows = Gather(feed_sems[0], ids, ebuf)
+    feed_sum = Scatter(feed_sems[1], ids, own, feed_bufs)
+    attn_rows = Gather(attn_sems[0], ids, fbuf)
+    attn_sum = Scatter(attn_sems[1], ids, own, attn_bufs)
     columns = heads * HD
     tiles = width // 256
-    total, own, dx1 = (work.at[pl.ds(i * unit_rows, unit_rows)] for i in range(3))
     top = depth - 1
     packed = is_packed(lengths_ref, 8 * half)
-    for part in range(2):
-        rows = pl.ds(part * half, half)
-        ebuf[rows, :] = cot_ref[rows, :]
-        feed.send(part)
-    loads.start(top, "wdown", "slope", "wup", "m", "g", "x1", "wout", "q", "k", "v", "lse")
+    loads.add("grad", [grad_hbm] * depth, ebuf)
+    loads.start(top, "m", "wup", "grad", "wdown", "slope", "x1", "wout", "q", "k", "v", "lse", "g")
     loads.start(top, "wq", "wk", "wv", "a", "o", "x")
     dxb[...] = cot_ref[...].astype(F32)
     small_ref[...] = jnp.zeros_like(small_ref)
@@ -799,30 +1165,46 @@
         note(4, jnp.sum(dxb[...], axis=0, keepdims=True))
         dkb[...] = jnp.zeros_like(dkb)
         dvb[...] = jnp.zeros_like(dvb)
-        loads.wait(layer, "wdown", "slope", "wup")
+        loads.wait(layer, "m", "wup")
+
+        def expand(step, carry):
+            rows = span((3 - step) * unit_rows, unit_rows)
+            gated, slope = gelu_parts(dot(mbuf[rows, :], wup[...]))
+            gb[rows, :] = gated.astype(BF)
+            gpb[rows, :] = slope.astype(BF)
+            return carry
+
+        lax.fori_loop(0, 2, expand, 0)
+        loads.wait(layer, "wdown", "slope")
+        if layer == top:
+            loads.wait(layer, "grad")
 
         def contract(step, carry):
-            feed.receive(step)
-            unit = jnp.where(step < 2, step, 5 - step)
+            if layer == top:
+                unit = jnp.where(step < 2, 3 - step, step - 2)
+            else:
+                feed_rows.receive(step)
+                unit = jnp.where(step < 2, step, 5 - step)
             rows = span(unit * unit_rows, unit_rows)
             grad = dot(ebuf[rows, :], wdown[...], NT)
             grad = (grad * gpb[rows, :].astype(F32)).astype(BF)
             dhb[rows, :] = grad
             total[...] = dot(grad, wup[...], NT)
-            feed.scatter(unit, total, own)
+            feed_sum.send(unit, total)
             return carry
 
         lax.fori_loop(0, 4, contract, 0)
-        loads.start(layer - 1, "wdown", "slope", "wup")
+        loads.start(layer - 1, "wdown", "slope")
         event("attn", layer + 1, "middle")
         event("up", layer + 1, "end")
         if layer < top:
-            attn.finish()
+            attn_rows.finish()
+            attn_sum.finish()
         shift_sum = jnp.zeros((1, width), F32)
         scale_sum = jnp.zeros((1, width), F32)
         for part in range(2):
             if part == 0:
-                loads.wait(layer, "m", "x1")
+                loads.wait(layer, "x1")
                 outer(mbuf, dhb, feed_grads.at[0])
                 event("up", layer, "start")
             else:
@@ -830,22 +1212,22 @@
                 outer(ebuf, gb, feed_grads.at[1])
                 event("down", layer, "start")
             rows = pl.ds(part * half, half)
-            grad = feed.collect(part, own)
+            grad = feed_sum.collect(part)
             hat, rstd = norm(x1b[rows, :])
             shift_sum += jnp.sum(grad, axis=0, keepdims=True)
             scale_sum += jnp.sum(grad * hat, axis=0, keepdims=True)
             after = dxb[rows, :]
             after = after + norm_back(grad * (1.0 + cond_ref[8 * layer : 8 * layer + 1, width:]), hat, rstd)
             dx1[rows, :] = after
-            fbuf[rows, :] = after.astype(BF)
-            attn.send(part)
+            fbuf[attn_rows.own(part), :] = after.astype(BF)
+            attn_rows.send(part)
         note(0, shift_sum)
         note(1, scale_sum)
-        loads.start(layer - 1, "m", "g", "x1")
+        loads.start(layer - 1, "m", "g", "x1", "wup")
         loads.wait(layer, "wout", "q", "k", "v", "lse")
 
         def attend(step, carry):
-            attn.receive(step)
+            attn_rows.receive(step)
             unit = jnp.where(step < 2, step, 5 - step)
             rows = span(unit * unit_rows, unit_rows)
             grad_out = dot(fbuf[rows, :], wout[...], NT).astype(BF)
@@ -885,7 +1267,7 @@
         load_turned(wq, wk, wqk)
 
         def spread(step, carry):
-            unit = 3 - step
+            unit = jnp.where(step < 2, 3 - step, step - 2)
             rows = span(unit * unit_rows, unit_rows)
             low, high = turn_back(dkb[rows, :], rows, 1.0)
             dqk[rows, 256:384] = low
@@ -893,7 +1275,7 @@
             values = dvb[rows, :].astype(BF)
             dvv[rows, :] = values
             total[...] = dot(dqk[rows, :], wqk[...]) + dot(values, wv[...])
-            attn.scatter(unit, total, own)
+            attn_sum.send(unit, total)
             return carry
 
         lax.fori_loop(0, 4, spread, 0)
@@ -929,13 +1311,15 @@
                 each.start()
             for each in stores:
                 each.wait()
-        feed.finish()
+        if layer < top:
+            feed_rows.finish()
+        feed_sum.finish()
         loads.wait(layer, "x")
         gain_sum = jnp.zeros((1, width), F32)
         bias_sum = jnp.zeros((1, width), F32)
         for part in range(2):
             rows = pl.ds(part * half, half)
-            grad = attn.collect(part, own)
+            grad = attn_sum.collect(part)
             hat, rstd = norm(xb[rows, :])
             gain_sum += jnp.sum(grad * hat, axis=0, keepdims=True)
             bias_sum += jnp.sum(grad, axis=0, keepdims=True)
@@ -944,8 +1328,8 @@
             )
             dxb[rows, :] = made
             if layer:
-                ebuf[rows, :] = made.astype(BF)
-                feed.send(part)
+                ebuf[feed_rows.own(part), :] = made.astype(BF)
+                feed_rows.send(part)
         note(2, gain_sum)
         note(3, bias_sum)
         loads.start(layer - 1, "x")
@@ -955,7 +1339,8 @@
             each.wait()
         tail(deep, spot, ids, sums, dxb, small_ref, temb_ref, work, dsb, tail_refs,
              sum_ref, vec_ref, store_sems)
-    attn.finish()
+    attn_rows.finish()
+    attn_sum.finish()
 
 
 def tail(deep, spot, ids, sums, dxb, small_ref, temb_ref, work, dsb, scratch, sum_ref, vec_ref,
@@ -1069,7 +1454,7 @@
     sum_store.wait()
 
 
-def backward(heads, deep, cotangent, gains, lengths, tables, weights, kept, joined):
+def backward(heads, deep, cotangent, grad_all, gains, lengths, tables, weights, kept, joined):
     depth = len(kept)
     block, width = cotangent.shape
     length = 4 * block
@@ -1078,12 +1463,15 @@
     part = width // (2 * deep) if deep else width
     half, quarter = width // 2, width // 4
     held = [[each[name] for name in SAVED] for each in kept]
-    scratch = [pltpu.SemaphoreType.DMA((6, 2))] * 4
-    scratch += [pltpu.SemaphoreType.DMA((6 + len(SAVED),)), pltpu.SemaphoreType.DMA((2,))]
+    scratch = [pltpu.SemaphoreType.DMA((3, 2))] * 8
+    scratch += [pltpu.SemaphoreType.DMA((7 + len(SAVED),)), pltpu.SemaphoreType.DMA((2,))]
     scratch += [pltpu.VMEM((columns, width), BF)] * 3
     scratch += [pltpu.VMEM(each.shape[1:], BF) for each in weights[1:4]]
-    scratch += [pltpu.VMEM(each.shape, each.dtype) for each in held[0]]
-    scratch += group_scratch(length, width) + group_scratch(length, width)
+    for name, each in zip(SAVED, held[0]):
+        shape = (length, units) if name in ("g", "slope") else each.shape
+        scratch.append(pltpu.VMEM(shape, each.dtype))
+    scratch += [pltpu.VMEM((length, width), BF)] * 2
+    scratch += scatter_scratch(length, width) + scatter_scratch(length, width)
     scratch += [
         pltpu.VMEM((512, width), BF),
         pltpu.VMEM((length, units), BF),
@@ -1136,7 +1524,7 @@
 
     operands = [cotangent, gains, lengths, *tables]
     in_specs = [vmem_spec()] * len(operands)
-    remote = [*joined, *weights, *[each for layer in held for each in layer]]
+    remote = [*joined, grad_all, *weights, *[each for layer in held for each in layer]]
     in_specs += [any_spec()] * len(remote)
     return pl.pallas_call(
         kernel,
@@ -1292,12 +1680,13 @@
     deep = 4 if lax.axis_size("dp") == 8 else 0
     weights = (jnp.swapaxes(w_qkv, 2, 3), w_out, w_up, w_down, w_ada)
     vectors = (ln_gain, ln_bias, b_down, b_ada, lengths, timesteps)
-    made, kept = forward(heads, tokens, w_self, vectors, weights)
-    (activations, estimate, conds, cosine, sine, temb) = made
+    made, kept = forward(heads, tokens, cotangent, w_self, vectors, weights)
+    (activations, estimate, conds, cosine, sine, temb, grad_all) = made
     made = backward(
         heads,
         deep,
         cotangent,
+        grad_all,
         ln_gain,
         lengths,
         (cosine, sine, temb, conds),

time: 364 us -> 349 us (0.959)
  Pallas kernels: 356 us -> 341 us
    pallas_call x1, Pallas kernels: 174 us -> 165 us  [forward(): pl.pallas_call(kernel, out_shape=out_shape, in_specs=[vmem_spec()] * len(...]
    pallas_call x1, Pallas kernels: 170 us -> 164 us  [backward(): pl.pallas_call(kernel, out_shape=out_shape, in_specs=in_specs, out_specs=...]
where the time goes in v1:
time: 349 us; the launch traced here: 344 us
  Pallas kernels  341 us (98%)
    pallas_call x1, Pallas kernels, forward(): pl.pallas_call(kernel, out_shape=out_shape, in_specs=[vmem_spec()] * len(...  165 us
    pallas_call x1, Pallas kernels, backward(): pl.pallas_call(kernel, out_shape=out_shape, in_specs=in_specs, out_specs=...  164 us
    pallas_call x1, Pallas kernels, finish(): pl.pallas_call(kernel, grid=(steps,), out_shape=[*[jax.ShapeDtypeStruct(e...  12.2 us

profile of v1, /device:TPU:5, one launch (start us, length us, event | category | flops | bytes accessed | tf_op | source)
XLA Modules:
  0.0 344.3 jit_solution(5081240968010032021)
XLA Ops:
  0.6 0.5 fusion.2.refs_6_
  1.2 0.6 multiply_exponential_fusion.refs_7_
  1.7 164.7 %layers_forward.1 = (bf16[256,768]{1,0:T(8,128)(2,1)}, bf16[256,768]{1,0:T(8,128)(2,1)}, f32[16,1536]{1,0:T(8,128)}, f32[1024,128]{1,0:T(8,128)}, f32[1024,128]{...) custom-call(f32[2,768]{1,0:T(2,128)} %refs_1_.4, ...), custom_call_target="tpu_custom_call" | custom-call | tf_op jit(solution)/shard_map/layers_forward/pallas_call | solution.py:991
  166.5 164.4 %layers_backward.1 = (f32[256,768]{1,0:T(8,128)}, f32[16,768]{1,0:T(8,128)}, f32[96,768]{1,0:T(8,128)}, f32[96,768]{1,0:T(8,128)}, f32[2,96,768]{2,1,0:T(8,128)}...) custom-call(bf16[256,768]{1,0:T(8,128)(2,1)} %refs_0_.3, ...), custom_call_target="tpu_custom_call" | custom-call | tf_op jit(solution)/shard_map/layers_backward/pallas_call | solution.py:1529
  330.9 0.0 copy-start
  330.9 12.2 %write_grads.1 = (f32[256,768]{1,0:T(8,128)}, f32[2,768]{1,0:T(2,128)}, f32[2,768]{1,0:T(2,128)}, f32[2,1536]{1,0:T(2,128)}, f32[2,768]{1,0:T(2,128)}, /*index=5...) custom-call(f32[256,768]{1,0:T(8,128)} %get-tuple-element.88.refs_0_, ...), custom_call_target="tpu_custom_call" | custom-call | tf_op jit(solution)/shard_map/write_grads/pallas_call | solution.py:1631
  343.1 0.0 copy-done
  343.1 0.7 copy.27
Async XLA Ops:
  330.9 12.2 %copy-start = (bf16[256,768]{1,0:T(8,128)(2,1)S(1)}, bf16[256,768]{1,0:T(8,128)(2,1)}, u32[]{:S(2)}) copy-start(bf16[256,768]{1,0:T(8,128)(2,1)} %get-tuple-element.118) | copy-start | bytes 1179652

commit v2 on v1

--- a/solution.py
+++ b/solution.py
@@ -105,10 +105,16 @@
     def near(self, part):
         self.sibling_copy(part).wait_recv()
 
-    def far(self, part):
+    def arrive(self, part):
         self.far_copy(part).wait_recv()
         self.forward_copy(part).start()
+
+    def settle(self, part):
         self.forward_copy(part).wait()
+
+    def far(self, part):
+        self.arrive(part)
+        self.settle(part)
 
     def receive(self, step):
         @pl.when(step < 2)
@@ -403,7 +409,7 @@
     return jnp.where(unit < 2, 0, 2) + half
 
 
-SAVED = ("a", "q", "k", "v", "o", "x1", "m", "g", "slope", "x", "lse")
+SAVED = ("a", "q", "k", "v", "o", "o2", "x1", "m", "g", "slope", "x", "lse")
 
 
 def forward_kernel(depth, heads, refs):
@@ -597,13 +603,13 @@
 
         lax.fori_loop(0, count, body, 0)
 
-    def attend_far(number, save, before):
+    def attend_far(number, save, count, pick, before):
         keys = pl.ds(length // 2, length // 2)
         layer, slot = number % depth, number % 2
 
         def body(step, carry):
             before(step)
-            shard, unit = by_unit(step)
+            shard, unit = pick(step)
             place = 2 * unit + shard
             rows = span(unit * unit_rows, unit_rows)
             attended = jnp.zeros((unit_rows, columns), F32)
@@ -633,7 +639,7 @@
 
             return carry
 
-        lax.fori_loop(0, 4, body, 0)
+        lax.fori_loop(0, count, body, 0)
 
     def feed(number, save, pick, before):
         layer = number % depth
@@ -669,48 +675,28 @@
         slot = number % 2
         made = []
         for part in range(2):
-            pairs = (
-                (
-                    ob2.at[slot, 1, pl.ds(part * unit_rows, unit_rows)],
-                    ob2.at[slot, 0, pl.ds((3 - part) * unit_rows, unit_rows)],
-                ),
-                (lse2.at[slot, 1, part], lse2.at[slot, 0, 3 - part]),
+            made.append(
+                pltpu.make_async_remote_copy(
+                    src_ref=lse2.at[slot, 1, part],
+                    dst_ref=lse2.at[slot, 0, 3 - part],
+                    send_sem=cross_send.at[2 * slot + part],
+                    recv_sem=cross_recv.at[2 * slot + part],
+                    device_id=ids[1],
+                    device_id_type=MESH,
+                )
             )
-            for kind, (src, dst) in enumerate(pairs):
-                place = 4 * slot + 2 * part + kind
-                made.append(
-                    pltpu.make_async_remote_copy(
-                        src_ref=src,
-                        dst_ref=dst,
-                        send_sem=cross_send.at[place],
-                        recv_sem=cross_recv.at[place],
-                        device_id=ids[1],
-                        device_id_type=MESH,
-                    )
-                )
-                made[-1].start()
+            made[-1].start()
         crossings[number] = made
 
     def late(number):
         slot = number % 2
         saved = saved_hbm[number % depth]
-        if number == depth:
-            for part in range(2):
-                grads.near(part)
-                grads.far(part)
-            store("grad", ebuf, grad_hbm)
         for part in range(2):
             mixes[slot].far(part)
         store("m", mbufs[slot], saved["m"])
         for each in crossings[number]:
             each.wait_recv()
-        store("o", ob2.at[slot, 0], saved["o"])
         store("lse", lse2.at[slot, 0], saved["lse"])
-
-    def steps_of(*pairs):
-        for index, count in pairs:
-            if index < len(fetches):
-                fetches[index].step(count)
 
     def events(table):
         def before(step):
@@ -761,7 +747,7 @@
                 made = norm(after)[0] * (1.0 + scale) + shift
                 mix_rows[pl.ds(2 * half * part, half), :] = made.astype(BF)
                 mix.sibling_copy(part).start()
-                if save:
+                if number == 2 * depth - 1:
                     mix.far_copy(part).start()
 
             return action
@@ -789,86 +775,94 @@
             near_a.drain()
             near_f.drain()
         stored("q", "k", "v")
-        if save:
+
+        def turn(shard):
+            rows = wa[layer].at[shard, part_a[0]], wa[layer].at[shard, part_a[1]]
+            load_turned(*rows, wqk[layer].at[shard])
+
+        far_table = {3: [after_attend(0)]}
+        feed_table = {
+            0: [mixed(0)],
+            1: [after_attend(1)],
+            2: [mixed(1)],
+            3: [after_feed(0)],
+        }
+        order = by_unit
+        if number == 0:
+            make_tables()
+            turn(0)
+            arrive = {
+                0: [near_rows(0)],
+                1: [near_rows(1)],
+                2: [(0, 2), waits(7), (1, 1), far_rows(0)],
+                3: [far_rows(1), waits(8), (2, 1)],
+            }
+
+            def in_order(step):
+                return jnp.where(step < 2, step, 5 - step)
+
+            project(number, 4, lambda step: (0, in_order(step)), events(arrive))
+            attend_near(number, 2, lambda step: (0, step), events({1: [(0, 3)]}))
+            make_cond(layer)
+            first = {1: [(1, 2), waits(9, 10, 11, 12), (3, 1)]}
+            attend_far(number, save, 2, lambda step: (0, step), events(first))
+            fetches[0].step(4)
+            turn(1)
+            second = {3: [(1, 3), (2, 2), waits(13), (4, 1)]}
+            project(number, 4, lambda step: (1, in_order(step)), events(second))
+            attend_near(number, 2, lambda step: (1, step), events({}))
+            far_table = {1: [after_attend(0)]}
+            attend_far(number, save, 2, lambda step: (1, step), events(far_table))
+            feed_table = {
+                0: [mixed(0), (2, 3), (3, 2), waits(14), (5, 1)],
+                1: [after_attend(1), mixed(1)],
+                2: [(1, 4), (3, 3), (4, 2), (2, 4)],
+                3: [after_feed(0)],
+            }
+            order = by_shard
+        else:
+            own_table = {0: [near_rows(0)], 1: [near_rows(1)]}
+            near_table = {3: [lambda: group.arrive(0)]}
+            if not save:
+                turn(0)
+                own_table[0] += [(base + 1, 3), (base + 2, 2)]
+                own_table[2] = [(base, 4), lambda: turn(1)]
+                near_table[3] = [(base + 2, 3), lambda: group.arrive(0)]
+                feed_table[0] += [(base + 1, 4)]
+                feed_table[1] += [(base + 2, 4)]
+            project(number, 4, by_shard, events(own_table))
+            attend_near(number, 4, by_unit, events(near_table))
+            if not save:
+                make_cond(layer)
             if number == depth:
+                for part in range(2):
+                    grads.near(part)
+                    grads.far(part)
+                store("grad", ebuf, grad_hbm)
+            arrive = {
+                0: [lambda: group.settle(0)],
+                1: [lambda: group.arrive(1)],
+                2: [lambda: group.settle(1)],
+            }
+            project(number, 4, lambda step: (lax.rem(step, 2), 3 - step // 2), events(arrive))
+            if number == depth - 1:
                 for part in range(2):
                     ebuf[grads.own(part), :] = cot_ref[pl.ds(part * half, half), :]
                     grads.send(part)
-            arrive = events({0: [near_rows(0)], 1: [near_rows(1)]})
-            project(number, 4, by_shard, arrive)
-            attend_near(number, 4, by_unit, events({}))
             if number > depth:
-                late(number - 1)
-            arrive = events({0: [far_rows(0)], 2: [far_rows(1)]})
-            project(number, 4, lambda step: (lax.rem(step, 2), 3 - step // 2), arrive)
-            store("a", abufs[slot], saved_hbm[layer]["a"])
-            store("x", xb, saved_hbm[layer]["x"])
-            for name, src in (("q", q2), ("k", k2), ("v", v2)):
-                store(name, src.at[0], saved_hbm[layer][name])
-            far_table = {3: [after_attend(0)]}
-            feed_table = {
-                0: [mixed(0)],
-                1: [after_attend(1)],
-                2: [mixed(1)],
-                3: [after_feed(0)],
-            }
-            order = by_unit
-        else:
-            if layer == 0:
-                make_tables()
-            load_turned(
-                wa[layer].at[0, part_a[0]], wa[layer].at[0, part_a[1]], wqk[layer].at[0]
-            )
-            rows_table = {
-                0: [near_rows(0)],
-                1: [near_rows(1)],
-                2: [far_rows(0)],
-                3: [far_rows(1)],
-            }
-            if layer == 0:
-                rows_table[2] = [(0, 2), far_rows(0)]
-                rows_table[3] = [far_rows(1), waits(7), (1, 1)]
-                first_near = {0: [(0, 3)]}
-                second_near = {1: [(1, 3)]}
-                far_table = {0: [(2, 2), waits(9, 10, 11, 12), (3, 1)], 3: [after_attend(0)]}
-                feed_table = {
-                    0: [mixed(0), (3, 2), waits(13), (4, 1)],
-                    1: [after_attend(1), mixed(1), (2, 3), (1, 4)],
-                    2: [(2, 4), (3, 3), (4, 2), waits(14), (5, 1)],
-                    3: [after_feed(0)],
-                }
-                order = by_shard
-            else:
-                rows_table[2] = [(base + 1, 3), *rows_table[2]]
-                rows_table[3] = [*rows_table[3], (base + 2, 2)]
-                first_near = {}
-                second_near = {0: [(base + 2, 3)]}
-                far_table = {3: [after_attend(0)]}
-                feed_table = {
-                    0: [mixed(0), (base + 1, 4)],
-                    1: [after_attend(1), (base + 2, 4)],
-                    2: [mixed(1)],
-                    3: [after_feed(0)],
-                }
-                order = by_unit
-
-            def in_order(step):
-                return jnp.where(step < 2, step, 5 - step)
-
-            project(number, 4, lambda step: (0, in_order(step)), events(rows_table))
-            attend_near(number, 2, lambda step: (0, step), events(first_near))
-            make_cond(layer)
-            if layer == 0:
-                events({0: [waits(8), (2, 1), (1, 2)]})(0)
-            events({0: [(base, 4)]})(0)
-            load_turned(
-                wa[layer].at[1, part_a[0]], wa[layer].at[1, part_a[1]], wqk[layer].at[1]
-            )
-            project(number, 4, lambda step: (1, in_order(step)), events({}))
-            attend_near(number, 2, lambda step: (1, step), events(second_near))
-        attend_far(number, save, events(far_table))
+                for part in range(2):
+                    mixes[(number - 1) % 2].far_copy(part).start()
+            if save:
+                store("a", abufs[slot], saved_hbm[layer]["a"])
+                store("x", xb, saved_hbm[layer]["x"])
+                for name, src in (("q", q2), ("k", k2), ("v", v2)):
+                    store(name, src.at[0], saved_hbm[layer][name])
+            attend_far(number, save, 4, by_unit, events(far_table))
         if save:
             cross(number)
+            rows = pl.ds(0, length // 2)
+            store("o", ob2.at[slot, 0, rows], saved_hbm[layer]["o"])
+            store("o2", ob2.at[slot, 1, rows], saved_hbm[layer]["o2"])
         stored("g", "slope")
         feed(number, save, order, events(feed_table))
         if save:
@@ -896,7 +890,8 @@
             run(number, between)
         else:
             run(number, enter(number + 1))
-    late(2 * depth - 1)
+    for number in range(depth, 2 * depth):
+        late(number)
     for each in gathers:
         each.finish()
     for each in (*mixes, grads):
@@ -935,7 +930,8 @@
         "q": ((length, 256), BF),
         "k": ((length, 256), BF),
         "v": ((length, columns), BF),
-        "o": ((length, columns), BF),
+        "o": ((length // 2, columns), BF),
+        "o2": ((length // 2, columns), BF),
         "x1": ((block, width), F32),
         "m": ((length, width), BF),
         "g": ((length // 2, units), BF),
@@ -956,7 +952,7 @@
     out_specs = [vmem_spec()] * 6 + [any_spec()] * (1 + depth * len(SAVED))
     dma = pltpu.SemaphoreType.DMA
     scratch = [dma((3, 2))] * 10
-    scratch += [dma((2, 2))] * 2 + [dma((3 * depth, 2, 6)), dma((8,)), dma((8,))]
+    scratch += [dma((2, 2))] * 2 + [dma((3 * depth, 2, 6)), dma((4,)), dma((4,))]
     scratch += [dma((4 + 6 * depth,)), dma((1 + depth * len(SAVED),))]
     scratch += [
         pltpu.VMEM((block, width), BF),
@@ -972,7 +968,7 @@
         pltpu.VMEM((2, length, 256), BF),
         pltpu.VMEM((2, length, 256), BF),
         pltpu.VMEM((2, length, columns), BF),
-        pltpu.VMEM((2, 2, length, columns), BF),
+        pltpu.VMEM((2, 2, length // 2, columns), BF),
         pltpu.VMEM((2, 2, 4, 8, block), F32),
         pltpu.VMEM((4, block, columns), F32),
         pltpu.VMEM((4, 2, block, 128), F32),
@@ -1074,7 +1070,7 @@
     if deep:
         sum_ref, vec_ref = take(2)
     feed_sems, attn_sems = [take(2), take(2)], [take(2), take(2)]
-    load_sems, store_sems = take(2)
+    load_sems, store_sems, out_sems = take(3)
     loads = Loads(load_sems)
     wq, wk, wv = (
         loads.add(name, [wqkv_hbm.at[layer, part] for layer in range(depth)], take(1)[0])
@@ -1085,13 +1081,16 @@
         for name, src in (("wout", wout_hbm), ("wup", wup_hbm), ("wdown", wdown_hbm))
     )
     buffers = dict(zip(SAVED, take(len(SAVED))))
+    outs = [take(2) for _ in range(depth)]
     for name in SAVED:
+        if name in ("o", "o2"):
+            continue
         rows = saved_hbm[0][name].shape[0]
         buffer = buffers[name]
         if rows < buffer.shape[0]:
             buffer = buffer.at[pl.ds(0, rows)]
         loads.add(name, [saved_hbm[layer][name] for layer in range(depth)], buffer)
-    abuf, qb, kb, vb, ob, x1b, mbuf, gb, gpb, xb, lse = (buffers[name] for name in SAVED)
+    abuf, qb, kb, vb, _, _, x1b, mbuf, gb, gpb, xb, lse = (buffers[name] for name in SAVED)
     ebuf, fbuf = take(2)
     feed_bufs, attn_bufs = take(6), take(6)
     (wqk, dhb, qmask, domask, dsb, pb, dkb, dvb, dqk, dvv, work, dxb) = take(12)
@@ -1132,7 +1131,40 @@
     packed = is_packed(lengths_ref, 8 * half)
     loads.add("grad", [grad_hbm] * depth, ebuf)
     loads.start(top, "m", "wup", "grad", "wdown", "slope", "x1", "wout", "q", "k", "v", "lse", "g")
-    loads.start(top, "wq", "wk", "wv", "a", "o", "x")
+    loads.start(top, "wq", "wk", "wv", "a", "x")
+    out_loads = []
+    out_sends = []
+    for layer in range(depth):
+        rows = outs[layer][0].at[pl.ds(0, 4 * half)]
+        pairs = ((saved_hbm[layer]["o"], rows), (saved_hbm[layer]["o2"], outs[layer][1]))
+        out_loads.append(
+            [
+                pltpu.make_async_copy(src, dst, out_sems.at[layer, 4 + i])
+                for i, (src, dst) in enumerate(pairs)
+            ]
+        )
+        out_sends.append(
+            [
+                pltpu.make_async_remote_copy(
+                    src_ref=outs[layer][1].at[pl.ds(part * unit_rows, unit_rows)],
+                    dst_ref=outs[layer][0].at[pl.ds((3 - part) * unit_rows, unit_rows)],
+                    send_sem=out_sems.at[layer, part],
+                    recv_sem=out_sems.at[layer, 2 + part],
+                    device_id=ids[1],
+                    device_id_type=MESH,
+                )
+                for part in range(2)
+            ]
+        )
+        for each in out_loads[layer]:
+            each.start()
+
+    def send_outs(layer):
+        out_loads[layer][1].wait()
+        for each in out_sends[layer]:
+            each.start()
+
+    send_outs(top)
     dxb[...] = cot_ref[...].astype(F32)
     small_ref[...] = jnp.zeros_like(small_ref)
 
@@ -1228,6 +1260,12 @@
 
         def attend(step, carry):
             attn_rows.receive(step)
+            if layer:
+
+                @pl.when(step == 3)
+                def _():
+                    send_outs(layer - 1)
+
             unit = jnp.where(step < 2, step, 5 - step)
             rows = span(unit * unit_rows, unit_rows)
             grad_out = dot(fbuf[rows, :], wout[...], NT).astype(BF)
@@ -1281,7 +1319,11 @@
         lax.fori_loop(0, 4, spread, 0)
         loads.start(layer - 1, "wq", "wk", "wv")
         event("down", layer, "middle")
-        loads.wait(layer, "a", "o")
+        loads.wait(layer, "a")
+        out_loads[layer][0].wait()
+        for each in out_sends[layer]:
+            each.wait()
+        ob = outs[layer][0]
         places = (
             turned_place(columns, 0, 4 * columns),
             turned_place(columns, columns, 4 * columns),
@@ -1300,7 +1342,7 @@
             return carry
 
         lax.fori_loop(0, tiles, attn_tile, 0)
-        loads.start(layer - 1, "a", "o")
+        loads.start(layer - 1, "a")
         event("attn", layer, "start")
         if not deep:
             stores = [
@@ -1465,11 +1507,13 @@
     held = [[each[name] for name in SAVED] for each in kept]
     scratch = [pltpu.SemaphoreType.DMA((3, 2))] * 8
     scratch += [pltpu.SemaphoreType.DMA((7 + len(SAVED),)), pltpu.SemaphoreType.DMA((2,))]
+    scratch += [pltpu.SemaphoreType.DMA((depth, 6))]
     scratch += [pltpu.VMEM((columns, width), BF)] * 3
     scratch += [pltpu.VMEM(each.shape[1:], BF) for each in weights[1:4]]
     for name, each in zip(SAVED, held[0]):
         shape = (length, units) if name in ("g", "slope") else each.shape
-        scratch.append(pltpu.VMEM(shape, each.dtype))
+        scratch.append(pltpu.VMEM((16, 128) if name in ("o", "o2") else shape, each.dtype))
+    scratch += [pltpu.VMEM((length, columns), BF), pltpu.VMEM((length // 2, columns), BF)] * depth
     scratch += [pltpu.VMEM((length, width), BF)] * 2
     scratch += scatter_scratch(length, width) + scatter_scratch(length, width)
     scratch += [

time: 349 us -> 344 us (0.986)
    pallas_call x1, Pallas kernels: 165 us -> 157 us  [forward(): pl.pallas_call(kernel, out_shape=out_shape, in_specs=[vmem_spec()] * len(...]
    pallas_call x1, Pallas kernels: 164 us -> 170 us  [backward(): pl.pallas_call(kernel, out_shape=out_shape, in_specs=in_specs, out_specs=...]
where the time goes in v2:
time: 344 us; the launch traced here: 342 us
  Pallas kernels  339 us (99%)
    pallas_call x1, Pallas kernels, backward(): pl.pallas_call(kernel, out_shape=out_shape, in_specs=in_specs, out_specs=...  170 us
    pallas_call x1, Pallas kernels, forward(): pl.pallas_call(kernel, out_shape=out_shape, in_specs=[vmem_spec()] * len(...  157 us
    pallas_call x1, Pallas kernels, finish(): pl.pallas_call(kernel, grid=(steps,), out_shape=[*[jax.ShapeDtypeStruct(e...  12.2 us

profile of v2, /device:TPU:5, one launch (start us, length us, event | category | flops | bytes accessed | tf_op | source)
XLA Modules:
  0.0 341.8 jit_solution(10776783955843493308)
XLA Ops:
  0.6 0.5 fusion.2.refs_6_
  1.2 0.6 multiply_exponential_fusion.refs_7_
  1.7 156.6 %layers_forward.1 = (bf16[256,768]{1,0:T(8,128)(2,1)}, bf16[256,768]{1,0:T(8,128)(2,1)}, f32[16,1536]{1,0:T(8,128)}, f32[1024,128]{1,0:T(8,128)}, f32[1024,128]{...) custom-call(f32[2,768]{1,0:T(2,128)} %refs_1_.4, ...), custom_call_target="tpu_custom_call" | custom-call | tf_op jit(solution)/shard_map/layers_forward/pallas_call | solution.py:987
  158.3 170.1 %layers_backward.1 = (f32[256,768]{1,0:T(8,128)}, f32[16,768]{1,0:T(8,128)}, f32[96,768]{1,0:T(8,128)}, f32[96,768]{1,0:T(8,128)}, f32[2,96,768]{2,1,0:T(8,128)}...) custom-call(bf16[256,768]{1,0:T(8,128)(2,1)} %refs_0_.3, ...), custom_call_target="tpu_custom_call" | custom-call | tf_op jit(solution)/shard_map/layers_backward/pallas_call | solution.py:1573
  328.4 0.0 copy-start
  328.4 12.2 %write_grads.1 = (f32[256,768]{1,0:T(8,128)}, f32[2,768]{1,0:T(2,128)}, f32[2,768]{1,0:T(2,128)}, f32[2,1536]{1,0:T(2,128)}, f32[2,768]{1,0:T(2,128)}, /*index=5...) custom-call(f32[256,768]{1,0:T(8,128)} %get-tuple-element.92.refs_0_, ...), custom_call_target="tpu_custom_call" | custom-call | tf_op jit(solution)/shard_map/write_grads/pallas_call | solution.py:1675
  340.6 0.0 copy-done
  340.6 0.7 copy.27
Async XLA Ops:
  328.4 12.2 %copy-start = (bf16[256,768]{1,0:T(8,128)(2,1)S(1)}, bf16[256,768]{1,0:T(8,128)(2,1)}, u32[]{:S(2)}) copy-start(bf16[256,768]{1,0:T(8,128)(2,1)} %get-tuple-element.122) | copy-start | bytes 1179652

commit v3 on v2

--- a/solution.py
+++ b/solution.py
@@ -1318,7 +1318,8 @@
 
         lax.fori_loop(0, 4, spread, 0)
         loads.start(layer - 1, "wq", "wk", "wv")
-        event("down", layer, "middle")
+        if layer:
+            event("down", layer, "middle")
         loads.wait(layer, "a")
         out_loads[layer][0].wait()
         for each in out_sends[layer]:
@@ -1343,7 +1344,8 @@
 
         lax.fori_loop(0, tiles, attn_tile, 0)
         loads.start(layer - 1, "a")
-        event("attn", layer, "start")
+        if layer:
+            event("attn", layer, "start")
         if not deep:
             stores = [
                 pltpu.make_async_copy(attn_grads, attn_outs[layer], store_sems.at[0]),
@@ -1422,6 +1424,7 @@
         out = dsb.at[pl.ds(0, half), lanes[side]]
         out[...] = work[span((1 - bit) * half, half), lanes[side]].astype(BF)
         firsts.append(ladder.copy(out, near_in.at[side], device))
+    sums["down", 0].middle()
     for each in vec_z:
         each.wait_recv()
     row_z = vecs.at[core, y, x]
@@ -1434,10 +1437,10 @@
         out = dsb.at[pl.ds(half, quarter), lanes[side]]
         out[...] = work[span(bit * half + (1 - bit2) * quarter, quarter), lanes[side]].astype(BF)
         seconds.append(ladder.copy(out, next_in.at[side], device))
+    sums["attn", 0].start()
     vec_x.wait_recv()
     plane = vecs.at[core, y]
     vec_y = ladder.copy(plane, plane, far)
-    sums["attn", 0].middle()
     thirds = []
     for side, ((_, bit), (_, bit2)) in enumerate(ways):
         seconds[side].wait_recv()
@@ -1476,6 +1479,7 @@
             lasts[side * (deep - 1) + ahead - 1].wait_recv()
         own = result.at[core, side, span(bit * half + bit2 * quarter, quarter)]
         backs.append(ladder.copy(own, own, device))
+    sums["attn", 0].middle()
     ends = []
     for side, ((device, bit), _) in enumerate(ways):
         backs[side].wait_recv()
@@ -1588,7 +1592,7 @@
     attn_refs = refs[4 : 4 + depth]
     feed_refs = refs[4 + depth : 4 + 2 * depth]
     (tokens_ref, gain_ref, bias_ref, bada_ref, bdown_ref) = refs[4 + 2 * depth : 9 + 2 * depth]
-    (qkv_ref, out_ref, ada_ref, up_ref, down_ref, self_ref) = refs[9 + 2 * depth :]
+    (qkv_ref, out_ref, ada_ref, up_ref, down_ref, self_ref, picked) = refs[9 + 2 * depth :]
     step = pl.program_id(0)
     members = vec_ref.shape[0] // (8 * depth)
     width = vec_ref.shape[1]
@@ -1600,15 +1604,22 @@
         return dot(wanted, vec_ref[...]).astype(BF)
 
     rows = ada_ref.shape[1]
-    times = pick(5)
+
+    @pl.when(step == 0)
+    def _():
+        picked[2 * depth] = pick(5)
+        for layer in range(depth):
+            for place in range(2):
+                picked[2 * layer + place] = pick(8 * layer + place)
+
     device = lax.broadcasted_iota(jnp.int32, (width, rows), 0)
     column = lax.broadcasted_iota(jnp.int32, (width, rows), 1)
     chosen = (device == column + step * rows).astype(F32).astype(BF)
-    times = dot(times, chosen).astype(BF)
+    times = dot(picked[2 * depth], chosen).astype(BF)
     for layer in range(depth):
         for place in range(2):
             ada_ref[layer, :, place * width : (place + 1) * width] = dot(
-                times, pick(8 * layer + place), TN
+                times, picked[2 * layer + place], TN
             )
     self_ref[:, : width // 2] = sum_ref[0].astype(F32)
     self_ref[:, width // 2 :] = sum_ref[1].astype(F32)
@@ -1696,6 +1707,9 @@
             fixed(*shard),
             fixed(*shard),
             pl.BlockSpec((rows, width), lambda step: (step, 0)),
+        ],
+        scratch_shapes=[
+            pltpu.VMEM((2 * depth + 1, vectors.shape[0] // (8 * depth), width), BF)
         ],
         compiler_params=pltpu.CompilerParams(vmem_limit_bytes=LIMIT),
         name="write_grads",

time: 344 us -> 328 us (0.953)
  Pallas kernels: 339 us -> 321 us
    pallas_call x1, Pallas kernels: 170 us -> 154 us  [backward(): pl.pallas_call(kernel, out_shape=out_shape, in_specs=in_specs, out_specs=...]
where the time goes in v3:
time: 328 us; the launch traced here: 324 us
  Pallas kernels  321 us (98%)
    pallas_call x1, Pallas kernels, forward(): pl.pallas_call(kernel, out_shape=out_shape, in_specs=[vmem_spec()] * len(...  157 us
    pallas_call x1, Pallas kernels, backward(): pl.pallas_call(kernel, out_shape=out_shape, in_specs=in_specs, out_specs=...  154 us
    pallas_call x1, Pallas kernels, finish(): pl.pallas_call(kernel, grid=(steps,), out_shape=[*[jax.ShapeDtypeStruct(e...  11 us

profile of v3, /device:TPU:5, one launch (start us, length us, event | category | flops | bytes accessed | tf_op | source)
XLA Modules:
  0.0 324.2 jit_solution(4573478919955333481)
XLA Ops:
  0.6 0.5 fusion.2.refs_6_
  1.2 0.6 multiply_exponential_fusion.refs_7_
  1.7 156.6 %layers_forward.1 = (bf16[256,768]{1,0:T(8,128)(2,1)}, bf16[256,768]{1,0:T(8,128)(2,1)}, f32[16,1536]{1,0:T(8,128)}, f32[1024,128]{1,0:T(8,128)}, f32[1024,128]{...) custom-call(f32[2,768]{1,0:T(2,128)} %refs_1_.4, ...), custom_call_target="tpu_custom_call" | custom-call | tf_op jit(solution)/shard_map/layers_forward/pallas_call | solution.py:987
  158.3 153.7 %layers_backward.1 = (f32[256,768]{1,0:T(8,128)}, f32[16,768]{1,0:T(8,128)}, f32[96,768]{1,0:T(8,128)}, f32[96,768]{1,0:T(8,128)}, f32[2,96,768]{2,1,0:T(8,128)}...) custom-call(bf16[256,768]{1,0:T(8,128)(2,1)} %refs_0_.3, ...), custom_call_target="tpu_custom_call" | custom-call | tf_op jit(solution)/shard_map/layers_backward/pallas_call | solution.py:1577
  312.0 0.0 copy-start
  312.0 11.0 %write_grads.1 = (f32[256,768]{1,0:T(8,128)}, f32[2,768]{1,0:T(2,128)}, f32[2,768]{1,0:T(2,128)}, f32[2,1536]{1,0:T(2,128)}, f32[2,768]{1,0:T(2,128)}, /*index=5...) custom-call(f32[256,768]{1,0:T(8,128)} %get-tuple-element.92.refs_0_, ...), custom_call_target="tpu_custom_call" | custom-call | tf_op jit(solution)/shard_map/write_grads/pallas_call | solution.py:1686
  323.0 0.0 copy-done
  323.0 0.7 copy.27
Async XLA Ops:
  312.0 11.0 %copy-start = (bf16[256,768]{1,0:T(8,128)(2,1)S(1)}, bf16[256,768]{1,0:T(8,128)(2,1)}, u32[]{:S(2)}) copy-start(bf16[256,768]{1,0:T(8,128)(2,1)} %get-tuple-element.122) | copy-start | bytes 1179652

commit v4 on v3

--- a/solution.py
+++ b/solution.py
@@ -825,9 +825,10 @@
             near_table = {3: [lambda: group.arrive(0)]}
             if not save:
                 turn(0)
-                own_table[0] += [(base + 1, 3), (base + 2, 2)]
+                own_table[0] += [(base + 1, 3)]
+                near_table[1] = [(base + 2, 2)]
                 own_table[2] = [(base, 4), lambda: turn(1)]
-                near_table[3] = [(base + 2, 3), lambda: group.arrive(0)]
+                far_table[0] = [(base + 2, 3)]
                 feed_table[0] += [(base + 1, 4)]
                 feed_table[1] += [(base + 2, 4)]
             project(number, 4, by_shard, events(own_table))

time: 328 us -> 322 us (0.982)
  Pallas kernels: 321 us -> 316 us
    pallas_call x1, Pallas kernels: 157 us -> 152 us  [forward(): pl.pallas_call(kernel, out_shape=out_shape, in_specs=[vmem_spec()] * len(...]
where the time goes in v4:
time: 322 us; the launch traced here: 319 us
  Pallas kernels  316 us (98%)
    pallas_call x1, Pallas kernels, backward(): pl.pallas_call(kernel, out_shape=out_shape, in_specs=in_specs, out_specs=...  154 us
    pallas_call x1, Pallas kernels, forward(): pl.pallas_call(kernel, out_shape=out_shape, in_specs=[vmem_spec()] * len(...  152 us
    pallas_call x1, Pallas kernels, finish(): pl.pallas_call(kernel, grid=(steps,), out_shape=[*[jax.ShapeDtypeStruct(e...  11 us

profile of v4, /device:TPU:5, one launch (start us, length us, event | category | flops | bytes accessed | tf_op | source)
XLA Modules:
  0.0 319.3 jit_solution(10117679440102771617)
XLA Ops:
  0.6 0.5 fusion.2.refs_6_
  1.2 0.6 multiply_exponential_fusion.refs_7_
  1.7 151.5 %layers_forward.1 = (bf16[256,768]{1,0:T(8,128)(2,1)}, bf16[256,768]{1,0:T(8,128)(2,1)}, f32[16,1536]{1,0:T(8,128)}, f32[1024,128]{1,0:T(8,128)}, f32[1024,128]{...) custom-call(f32[2,768]{1,0:T(2,128)} %refs_1_.4, ...), custom_call_target="tpu_custom_call" | custom-call | tf_op jit(solution)/shard_map/layers_forward/pallas_call | solution.py:988
  153.3 153.8 %layers_backward.1 = (f32[256,768]{1,0:T(8,128)}, f32[16,768]{1,0:T(8,128)}, f32[96,768]{1,0:T(8,128)}, f32[96,768]{1,0:T(8,128)}, f32[2,96,768]{2,1,0:T(8,128)}...) custom-call(bf16[256,768]{1,0:T(8,128)(2,1)} %refs_0_.3, ...), custom_call_target="tpu_custom_call" | custom-call | tf_op jit(solution)/shard_map/layers_backward/pallas_call | solution.py:1578
  307.1 0.0 copy-start
  307.1 11.0 %write_grads.1 = (f32[256,768]{1,0:T(8,128)}, f32[2,768]{1,0:T(2,128)}, f32[2,768]{1,0:T(2,128)}, f32[2,1536]{1,0:T(2,128)}, f32[2,768]{1,0:T(2,128)}, /*index=5...) custom-call(f32[256,768]{1,0:T(8,128)} %get-tuple-element.92.refs_0_, ...), custom_call_target="tpu_custom_call" | custom-call | tf_op jit(solution)/shard_map/write_grads/pallas_call | solution.py:1687
  318.1 0.0 copy-done
  318.1 0.7 copy.27
Async XLA Ops:
  307.1 11.0 %copy-start = (bf16[256,768]{1,0:T(8,128)(2,1)S(1)}, bf16[256,768]{1,0:T(8,128)(2,1)}, u32[]{:S(2)}) copy-start(bf16[256,768]{1,0:T(8,128)(2,1)} %get-tuple-element.122) | copy-start | bytes 1179652

commit v5 on v4

--- a/solution.py
+++ b/solution.py
@@ -816,8 +816,8 @@
             feed_table = {
                 0: [mixed(0), (2, 3), (3, 2), waits(14), (5, 1)],
                 1: [after_attend(1), mixed(1)],
-                2: [(1, 4), (3, 3), (4, 2), (2, 4)],
-                3: [after_feed(0)],
+                2: [(1, 4), (2, 4)],
+                3: [(3, 3), (4, 2), after_feed(0)],
             }
             order = by_shard
         else:

time: 322 us -> 322 us (level)
  no operation moved by 1% of the time
where the time goes in v5:
time: 322 us; the launch traced here: 319 us
  Pallas kernels  316 us (98%)
    pallas_call x1, Pallas kernels, backward(): pl.pallas_call(kernel, out_shape=out_shape, in_specs=in_specs, out_specs=...  154 us
    pallas_call x1, Pallas kernels, forward(): pl.pallas_call(kernel, out_shape=out_shape, in_specs=[vmem_spec()] * len(...  152 us
    pallas_call x1, Pallas kernels, finish(): pl.pallas_call(kernel, grid=(steps,), out_shape=[*[jax.ShapeDtypeStruct(e...  11 us

profile of v5, /device:TPU:5, one launch (start us, length us, event | category | flops | bytes accessed | tf_op | source)
XLA Modules:
  0.0 319.3 jit_solution(4497034270764706244)
XLA Ops:
  0.6 0.5 fusion.2.refs_6_
  1.2 0.6 multiply_exponential_fusion.refs_7_
  1.7 151.5 %layers_forward.1 = (bf16[256,768]{1,0:T(8,128)(2,1)}, bf16[256,768]{1,0:T(8,128)(2,1)}, f32[16,1536]{1,0:T(8,128)}, f32[1024,128]{1,0:T(8,128)}, f32[1024,128]{...) custom-call(f32[2,768]{1,0:T(2,128)} %refs_1_.4, ...), custom_call_target="tpu_custom_call" | custom-call | tf_op jit(solution)/shard_map/layers_forward/pallas_call | solution.py:988
  153.3 153.8 %layers_backward.1 = (f32[256,768]{1,0:T(8,128)}, f32[16,768]{1,0:T(8,128)}, f32[96,768]{1,0:T(8,128)}, f32[96,768]{1,0:T(8,128)}, f32[2,96,768]{2,1,0:T(8,128)}...) custom-call(bf16[256,768]{1,0:T(8,128)(2,1)} %refs_0_.3, ...), custom_call_target="tpu_custom_call" | custom-call | tf_op jit(solution)/shard_map/layers_backward/pallas_call | solution.py:1578
  307.1 0.0 copy-start
  307.1 11.0 %write_grads.1 = (f32[256,768]{1,0:T(8,128)}, f32[2,768]{1,0:T(2,128)}, f32[2,768]{1,0:T(2,128)}, f32[2,1536]{1,0:T(2,128)}, f32[2,768]{1,0:T(2,128)}, /*index=5...) custom-call(f32[256,768]{1,0:T(8,128)} %get-tuple-element.92.refs_0_, ...), custom_call_target="tpu_custom_call" | custom-call | tf_op jit(solution)/shard_map/write_grads/pallas_call | solution.py:1687
  318.1 0.0 copy-done
  318.1 0.7 copy.27
Async XLA Ops:
  307.1 11.0 %copy-start = (bf16[256,768]{1,0:T(8,128)(2,1)S(1)}, bf16[256,768]{1,0:T(8,128)(2,1)}, u32[]{:S(2)}) copy-start(bf16[256,768]{1,0:T(8,128)(2,1)} %get-tuple-element.122) | copy-start | bytes 1179652
